TPU v7x, 32 devices: a whole 2x2x4 slice. The times are simulated.
32 devices in a mesh: seq: 2 (over core), row: 4 (over y, x), col: 4 (over z).
Axes of the slice: x: 2, y: 2, z: 4, core: 2. Of those that a mesh axis runs over, the one named last changes fastest.
Arguments:
- layer_in: bfloat16 [2, 1024, 2048], P(None, ('seq', 'col'), 'row'), may hold values from -6 to 6
- per_layer_in: bfloat16 [2, 1024, 256], P(None, ('seq', 'col')), may hold values from -6 to 6
- doc_lengths: int32 [2, 4], replicated, may hold values from 1 to 512, 1024 in all within a row
- w_query: bfloat16 [2048, 2048], P('row', 'col'), may hold values from -0.125 to 0.125
- w_key: bfloat16 [2048, 512], P('row', 'col'), may hold values from -0.125 to 0.125
- w_value: bfloat16 [2048, 512], P('row', 'col'), may hold values from -0.125 to 0.125
- w_out: bfloat16 [2048, 2048], P('col', 'row'), may hold values from -0.125 to 0.125
- w_gate: bfloat16 [2048, 8192], P('row', 'col'), may hold values from -0.125 to 0.125
- w_up: bfloat16 [2048, 8192], P('row', 'col'), may hold values from -0.125 to 0.125
- w_down: bfloat16 [8192, 2048], P('col', 'row'), may hold values from -0.0625 to 0.0625
- laurel_left: bfloat16 [2048, 64], P('row'), may hold values from -0.125 to 0.125
- laurel_right: bfloat16 [64, 2048], P(None, 'row'), may hold values from -0.75 to 0.75
- per_gate: bfloat16 [2048, 256], P('row'), may hold values from -0.125 to 0.125
- per_proj: bfloat16 [256, 2048], P(None, 'row'), may hold values from -0.375 to 0.375
- norm_gains: float32 [6, 2048], P(None, 'row'), may hold values from 0.5 to 1.5
- head_gains: float32 [2, 256], replicated, may hold values from 0.25 to 0.4
- out_grad: bfloat16 [2, 1024, 2048], P(None, ('seq', 'col'), 'row'), may hold values from -6 to 6
Outputs:
- layer_out: bfloat16 [2, 1024, 2048], P(None, ('seq', 'col'), 'row')
- grad_in: bfloat16 [2, 1024, 2048], P(None, ('seq', 'col'), 'row')
- grad_w_query: float32 [2048, 2048], P('row', 'col')
- grad_w_key: float32 [2048, 512], P('row', 'col')
- grad_w_value: float32 [2048, 512], P('row', 'col')
- grad_w_out: float32 [2048, 2048], P('col', 'row')
- grad_w_gate: float32 [2048, 8192], P('row', 'col')
- grad_w_up: float32 [2048, 8192], P('row', 'col')
- grad_w_down: float32 [8192, 2048], P('col', 'row')
- grad_laurel_left: float32 [2048, 64], P('row')
- grad_laurel_right: float32 [64, 2048], P(None, 'row')
- grad_per_gate: float32 [2048, 256], P('row')
- grad_per_proj: float32 [256, 2048], P(None, 'row')
- grad_norm_gains: float32 [6, 2048], P(None, 'row')
- grad_head_gains: float32 [2, 256], replicated
- clipped_gains: float32 [2, 8, 256], replicated
Inputs may be any that keep to these rules, and one draw needn't show every extreme that they name: `doc_lengths`: each row lists the lengths of one sequence's documents in order; they sum to 1024 and the longest is exactly 512.
All inputs are finite; a program needn't handle non-finite values.
Results may differ from a plain program's by a relative error of at most 0.017.
Values may be sent and summed in bfloat16 or wider, within the bound.
A program may use at most 128 MiB of HBM per device.

v0:
```python
import math

import jax
import jax.numpy as jnp
from jax import lax
from jax.experimental import pallas as pl
from jax.experimental.pallas import tpu as pltpu
from jax.sharding import PartitionSpec as P

EPSILON = 1e-06
CLIP_LEVEL = 3.0
ROPE_BASE = 1000000.0
ROOT_HALF = 0.7071067811865476
MASK_FILL = -1e30
MESH = pl.DeviceIdType.MESH
BF = jnp.bfloat16
F32 = jnp.float32
VMEM_BYTES = 63 * 2**20
PIECES = 4


def swapped(value, axis, apart):
    mask = 2**apart
    pairs = [(source, source ^ mask) for source in range(lax.axis_size(axis))]
    return lax.ppermute(value, axis, pairs)


def width_total(values):
    return lax.psum(values, "row")


def gather_tokens(values):
    return lax.all_gather(values, "col", axis=1, tiled=True)


def spread_rows(values, project):
    gathered = gather_tokens(values)
    return (gathered, lax.psum_scatter(project(gathered), "row", scatter_dimension=1, tiled=True))


def spread_cols(values, project):
    gathered = lax.all_gather(values, "row", axis=1, tiled=True)
    return (gathered, lax.psum_scatter(project(gathered), "col", scatter_dimension=1, tiled=True))


def times_right(left_side, right_side):
    return jnp.einsum("std,dn->stn", left_side, right_side, preferred_element_type=jnp.float32)


def times_back(left_side, right_side):
    return jnp.einsum("stn,dn->std", left_side, right_side, preferred_element_type=jnp.float32)


def outer_sum(left_side, right_side):
    return jnp.einsum("std,stn->dn", left_side, right_side, preferred_element_type=jnp.float32)


def norm_forward(values, gain_vec, width_all):
    square_sum = width_total(jnp.sum(values * values, axis=-1, keepdims=True))
    factor = lax.rsqrt(square_sum / width_all + EPSILON)
    normed = values * factor
    return (normed * gain_vec, normed, factor)


def norm_backward(grad_values, normed, factor, gain_vec, width_all):
    grad_normed = grad_values * gain_vec
    inner_sum = width_total(jnp.sum(grad_normed * normed, axis=-1, keepdims=True))
    result = factor * (grad_normed - normed * (inner_sum / width_all))
    return (result, jnp.sum(grad_values * normed, axis=(0, 1)))


def head_norm(values, gain_vec):
    return (
        values * lax.rsqrt(jnp.mean(values * values, axis=-1, keepdims=True) + EPSILON) * gain_vec
    )


def rotation(position, width_all):
    half_width = width_all // 2
    frequency = ROPE_BASE ** (-2.0 * jnp.arange(half_width, dtype=jnp.float32) / width_all)
    angles = position.astype(jnp.float32)[..., None] * frequency
    cosine_table = jnp.concatenate([jnp.cos(angles), jnp.cos(angles)], axis=-1)
    sine_table = jnp.concatenate([jnp.sin(angles), jnp.sin(angles)], axis=-1)
    return (cosine_table, sine_table)


def rotate(values, cosine_table, sine_table):
    half_width = values.shape[-1] // 2
    turned = jnp.concatenate([-values[..., half_width:], values[..., :half_width]], axis=-1)
    return values * cosine_table + turned * sine_table


def doc_places(doc_lengths, first_place, place_count):
    upto = jnp.tril(jnp.ones((doc_lengths.shape[1], doc_lengths.shape[1]), jnp.int32))
    doc_ends = jnp.sum(doc_lengths[:, None, :] * upto[None], axis=2)
    places = first_place + jnp.arange(place_count, dtype=jnp.int32)
    before = (doc_ends[:, None, :] <= places[None, :, None]).astype(jnp.int32)
    segment = jnp.sum(before, axis=2)
    doc_start = jnp.sum(before * doc_lengths[:, None, :], axis=2)
    return (segment, places, places[None, :] - doc_start)


def block_scores(queries, keys_all, block_start, block_size, query_seg, query_place, key_seg):
    keys_part = lax.dynamic_slice_in_dim(keys_all, block_start, block_size, 1)
    scores = jnp.einsum("sqhd,skd->shqk", queries, keys_part, preferred_element_type=jnp.float32)
    seg_part = lax.dynamic_slice_in_dim(key_seg, block_start, block_size, 1)
    key_place = block_start + jnp.arange(block_size, dtype=jnp.int32)
    allowed = (query_seg[:, None, :, None] == seg_part[:, None, None, :]) & (
        key_place[None, None, None, :] <= query_place[None, None, :, None]
    )
    return (scores, allowed)


def body_any(
    layer_in,
    per_layer_in,
    doc_lengths,
    w_query,
    w_key,
    w_value,
    w_out,
    w_gate,
    w_up,
    w_down,
    laurel_left,
    laurel_right,
    per_gate,
    per_proj,
    norm_gains,
    head_gains,
    out_grad,
):
    seq_count = layer_in.shape[0]
    width_all = layer_in.shape[2] * lax.axis_size("row")
    head_dim = head_gains.shape[1]
    heads_here = w_query.shape[1] // head_dim
    heads_all = heads_here * lax.axis_size("col")
    key_width = w_key.shape[1]
    ff_here = w_gate.shape[1]
    local_len = layer_in.shape[1] * lax.axis_size("col")
    tokens_row = local_len // lax.axis_size("row")
    seq_len = local_len * lax.axis_size("seq")
    col_index = lax.axis_index("col")
    even_col = col_index % 2 == 0
    q_width = heads_here * head_dim
    partner_key, partner_value = swapped((w_key, w_value), "col", 0)
    key_head = jnp.where(
        even_col,
        jnp.concatenate([w_key, partner_key], axis=1),
        jnp.concatenate([partner_key, w_key], axis=1),
    )
    value_head = jnp.where(
        even_col,
        jnp.concatenate([w_value, partner_value], axis=1),
        jnp.concatenate([partner_value, w_value], axis=1),
    )
    w_heads = jnp.concatenate([w_query, key_head, value_head], axis=1)
    w_back = jnp.concatenate([w_query, w_key, w_value], axis=1)
    w_gate_up = jnp.concatenate([w_gate, w_up], axis=1)
    inputs = layer_in.astype(jnp.float32)
    x_norm, x_normed, x_factor = norm_forward(inputs, norm_gains[0], width_all)
    x_low = x_norm.astype(jnp.bfloat16)
    x_rows, head_raw = spread_rows(x_low, lambda gathered: times_right(gathered, w_heads))
    q_raw = head_raw[:, :, :q_width].reshape(seq_count, tokens_row, heads_here, head_dim)
    k_raw = head_raw[:, :, q_width : q_width + head_dim]
    v_raw = head_raw[:, :, q_width + head_dim :]
    query_seg, query_place, query_pos = doc_places(
        doc_lengths, lax.axis_index(("seq", "row")) * tokens_row, tokens_row
    )
    key_seg, unused_place, unused_pos = doc_places(doc_lengths, 0, seq_len)
    cosine_table, sine_table = rotation(query_pos, head_dim)

    def query_prep(raw_part, gain_vec):
        return rotate(
            head_norm(raw_part, gain_vec), cosine_table[:, :, None], sine_table[:, :, None]
        )

    def key_prep(raw_part, gain_vec):
        return rotate(head_norm(raw_part, gain_vec), cosine_table, sine_table)

    def value_prep(raw_part):
        return head_norm(raw_part, 1.0)

    q_rot, query_back = jax.vjp(query_prep, q_raw, head_gains[0])
    k_rot, key_back = jax.vjp(key_prep, k_raw, head_gains[1])
    v_normed, value_back = jax.vjp(value_prep, v_raw)
    q_low = q_rot.astype(jnp.bfloat16)
    keys_all, values_all = (
        lax.all_gather(k_rot.astype(jnp.bfloat16), ("seq", "row"), axis=1, tiled=True),
        lax.all_gather(v_normed.astype(jnp.bfloat16), ("seq", "row"), axis=1, tiled=True),
    )
    block_size = min(512, seq_len)
    block_count = seq_len // block_size
    blocks = jnp.arange(block_count, dtype=jnp.int32)

    def scored(block_index):
        return block_scores(
            q_low, keys_all, block_index * block_size, block_size, query_seg, query_place, key_seg
        )

    def values_at(block_index):
        return lax.dynamic_slice_in_dim(values_all, block_index * block_size, block_size, 1)

    def stats_step(carry, block_index):
        row_top, row_total = carry
        scores, allowed = scored(block_index)
        new_top = jnp.maximum(row_top, jnp.max(jnp.where(allowed, scores, MASK_FILL), axis=3))
        weights = jnp.where(allowed, jnp.exp(scores - new_top[..., None]), 0.0)
        row_total = row_total * jnp.exp(row_top - new_top) + jnp.sum(weights, axis=3)
        return ((new_top, row_total), None)

    start_top = jnp.full((seq_count, heads_here, tokens_row), MASK_FILL, jnp.float32)
    (row_top, row_total), unused = lax.scan(
        stats_step, (start_top, jnp.zeros_like(start_top)), blocks
    )
    log_total = row_top + jnp.log(row_total)

    def probs_at(block_index):
        scores, allowed = scored(block_index)
        return jnp.where(allowed, jnp.exp(scores - log_total[..., None]), 0.0)

    def out_step(total_out, block_index):
        probs_low = probs_at(block_index).astype(jnp.bfloat16)
        total_out = total_out + jnp.einsum(
            "shqk,skd->sqhd", probs_low, values_at(block_index), preferred_element_type=jnp.float32
        )
        return (total_out, None)

    attended, unused = lax.scan(
        out_step, jnp.zeros((seq_count, tokens_row, heads_here, head_dim), jnp.float32), blocks
    )
    o_low = attended.astype(jnp.bfloat16).reshape(seq_count, tokens_row, q_width)
    head_slots = lax.dynamic_update_slice_in_dim(
        jnp.full((heads_all,), MASK_FILL, jnp.float32),
        jnp.max(row_top, axis=(0, 2)),
        col_index * heads_here,
        0,
    )
    logit_top = lax.pmax(head_slots, ("seq", "row", "col"))
    o_rows, attn_val = spread_cols(o_low, lambda gathered: times_right(gathered, w_out))
    attn_norm, attn_normed, attn_factor = norm_forward(attn_val, norm_gains[1], width_all)
    h_one = inputs + attn_norm
    lr_low = width_total(times_right(x_low, laurel_left)).astype(jnp.bfloat16)
    lo_val = times_right(lr_low, laurel_right)
    lo_norm, lo_normed, lo_factor = norm_forward(lo_val, norm_gains[2], width_all)
    h_two = (h_one + (x_norm + lo_norm)) * ROOT_HALF
    f_norm, f_normed, f_factor = norm_forward(h_two, norm_gains[3], width_all)
    f_low = f_norm.astype(jnp.bfloat16)
    f_rows, gate_up = spread_rows(f_low, lambda gathered: times_right(gathered, w_gate_up))
    gate_val = gate_up[:, :, :ff_here]
    up_val = gate_up[:, :, ff_here:]

    def geglu(gate_part, up_part):
        return jax.nn.gelu(gate_part, approximate=True) * up_part

    hidden, geglu_back = jax.vjp(geglu, gate_val, up_val)
    hid_low = hidden.astype(jnp.bfloat16)
    hid_rows, ff_val = spread_cols(hid_low, lambda gathered: times_right(gathered, w_down))
    ff_norm, ff_normed, ff_factor = norm_forward(ff_val, norm_gains[4], width_all)
    h_three = h_two + ff_norm
    h_low = h_three.astype(jnp.bfloat16)
    pg_val = width_total(times_right(h_low, per_gate))
    per_input = per_layer_in.astype(jnp.float32)

    def per_mix(gate_part):
        return jax.nn.gelu(gate_part, approximate=True) * per_input

    gp_val, per_back = jax.vjp(per_mix, pg_val)
    gp_low = gp_val.astype(jnp.bfloat16)
    pp_val = times_right(gp_low, per_proj)
    pp_norm, pp_normed, pp_factor = norm_forward(pp_val, norm_gains[5], width_all)
    layer_out = (h_three + pp_norm).astype(jnp.bfloat16)
    grad_top = out_grad.astype(jnp.float32)
    d_pp, gain_five = norm_backward(grad_top, pp_normed, pp_factor, norm_gains[5], width_all)
    d_pp_low = d_pp.astype(jnp.bfloat16)
    grad_per_proj = outer_sum(gp_low, d_pp_low)
    (d_pg,) = per_back(width_total(times_back(d_pp_low, per_proj)))
    d_pg_low = d_pg.astype(jnp.bfloat16)
    grad_per_gate = outer_sum(h_low, d_pg_low)
    d_three = grad_top + times_back(d_pg_low, per_gate)
    d_ff, gain_four = norm_backward(d_three, ff_normed, ff_factor, norm_gains[4], width_all)
    d_ff_low = d_ff.astype(jnp.bfloat16)
    dff_rows, d_hidden = spread_rows(d_ff_low, lambda gathered: times_back(gathered, w_down))
    grad_down = outer_sum(hid_rows, dff_rows)
    d_gate, d_up = geglu_back(d_hidden)
    d_gate_up = jnp.concatenate([d_gate, d_up], axis=2).astype(jnp.bfloat16)
    dgu_rows, d_f_low = spread_cols(d_gate_up, lambda gathered: times_back(gathered, w_gate_up))
    grad_gate_up = outer_sum(f_rows, dgu_rows)
    d_f, gain_three = norm_backward(d_f_low, f_normed, f_factor, norm_gains[3], width_all)
    d_half = (d_three + d_f) * ROOT_HALF
    d_lo, gain_two = norm_backward(d_half, lo_normed, lo_factor, norm_gains[2], width_all)
    d_lo_low = d_lo.astype(jnp.bfloat16)
    grad_laurel_right = outer_sum(lr_low, d_lo_low)
    d_lr_low = width_total(times_back(d_lo_low, laurel_right)).astype(jnp.bfloat16)
    grad_laurel_left = outer_sum(x_low, d_lr_low)
    d_attn, gain_one = norm_backward(d_half, attn_normed, attn_factor, norm_gains[1], width_all)
    d_attn_low = d_attn.astype(jnp.bfloat16)
    dattn_rows, d_o = spread_rows(d_attn_low, lambda gathered: times_back(gathered, w_out))
    grad_w_out = outer_sum(o_rows, dattn_rows)
    d_o_low = d_o.astype(jnp.bfloat16).reshape(seq_count, tokens_row, heads_here, head_dim)

    def delta_step(total_delta, block_index):
        d_probs = jnp.einsum(
            "sqhd,skd->shqk", d_o_low, values_at(block_index), preferred_element_type=jnp.float32
        )
        return (total_delta + jnp.sum(probs_at(block_index) * d_probs, axis=3), None)

    row_delta, unused = lax.scan(delta_step, jnp.zeros_like(log_total), blocks)

    def grad_step(carry, block_index):
        d_query, d_keys, d_values = carry
        block_start = block_index * block_size
        prob_vals = probs_at(block_index)
        d_probs = jnp.einsum(
            "sqhd,skd->shqk", d_o_low, values_at(block_index), preferred_element_type=jnp.float32
        )
        d_scores = (prob_vals * (d_probs - row_delta[..., None])).astype(jnp.bfloat16)
        keys_part = lax.dynamic_slice_in_dim(keys_all, block_start, block_size, 1)
        d_query = d_query + jnp.einsum(
            "shqk,skd->sqhd", d_scores, keys_part, preferred_element_type=jnp.float32
        )
        key_part = jnp.einsum("shqk,sqhd->skd", d_scores, q_low, preferred_element_type=jnp.float32)
        value_part = jnp.einsum(
            "shqk,sqhd->skd",
            prob_vals.astype(jnp.bfloat16),
            d_o_low,
            preferred_element_type=jnp.float32,
        )
        d_keys = lax.dynamic_update_slice_in_dim(d_keys, key_part, block_start, 1)
        d_values = lax.dynamic_update_slice_in_dim(d_values, value_part, block_start, 1)
        return ((d_query, d_keys, d_values), None)

    zero_keys = jnp.zeros((seq_count, seq_len, head_dim), jnp.float32)
    (d_query, d_keys, d_values), unused = lax.scan(
        grad_step, (jnp.zeros_like(attended), zero_keys, zero_keys), blocks
    )
    own_keys, own_values = (
        lax.psum_scatter(d_keys, ("seq", "row"), scatter_dimension=1, tiled=True),
        lax.psum_scatter(d_values, ("seq", "row"), scatter_dimension=1, tiled=True),
    )
    pair_keys, pair_values = swapped((own_keys, own_values), "col", 0)
    d_q_raw, d_q_gain = query_back(d_query)
    d_k_raw, d_k_gain = key_back(own_keys + pair_keys)
    (d_v_raw,) = value_back(own_values + pair_values)
    key_offset = col_index % 2 * key_width
    d_heads_low = jnp.concatenate(
        [
            d_q_raw.reshape(seq_count, tokens_row, q_width),
            lax.dynamic_slice_in_dim(d_k_raw, key_offset, key_width, 2),
            lax.dynamic_slice_in_dim(d_v_raw, key_offset, key_width, 2),
        ],
        axis=2,
    ).astype(jnp.bfloat16)
    dhead_rows, d_x_heads = spread_cols(d_heads_low, lambda gathered: times_back(gathered, w_back))
    grad_heads = outer_sum(x_rows, dhead_rows)
    d_x_low = d_x_heads + times_back(d_lr_low, laurel_left)
    d_x_part, gain_zero = norm_backward(
        d_half + d_x_low, x_normed, x_factor, norm_gains[0], width_all
    )
    grad_in = (d_half + d_x_part).astype(jnp.bfloat16)
    head_part = width_total(jnp.stack([d_q_gain, d_k_gain * 0.5]))
    sum_heads, sum_out, sum_gate_up, sum_down = lax.psum(
        (grad_heads, grad_w_out, grad_gate_up, grad_down), "seq"
    )
    sum_left, sum_right, sum_per_gate, sum_per_proj, sum_gains, sum_head_gains = lax.psum(
        (
            grad_laurel_left,
            grad_laurel_right,
            grad_per_gate,
            grad_per_proj,
            jnp.stack([gain_zero, gain_one, gain_two, gain_three, gain_four, gain_five]),
            head_part,
        ),
        ("seq", "col"),
    )
    clip_factor = jnp.sqrt(CLIP_LEVEL / jnp.maximum(logit_top, CLIP_LEVEL))
    clipped_gains = jnp.stack(
        [
            clip_factor[:, None] * head_gains[0][None, :],
            clip_factor[:, None] * head_gains[1][None, :],
        ]
    )
    return (
        layer_out,
        grad_in,
        sum_heads[:, :q_width],
        sum_heads[:, q_width : q_width + key_width],
        sum_heads[:, q_width + key_width :],
        sum_out,
        sum_gate_up[:, :ff_here],
        sum_gate_up[:, ff_here:],
        sum_down,
        sum_left,
        sum_right,
        sum_per_gate,
        sum_per_proj,
        sum_gains,
        sum_head_gains,
        clipped_gains,
    )


def group_gather(values):
    return lax.all_gather(values, ("seq", "col"), axis=0, tiled=True)


def group_scatter(partial):
    return lax.psum_scatter(
        partial.astype(jnp.bfloat16), ("seq", "col"), scatter_dimension=0, tiled=True
    ).astype(jnp.float32)


def to_owner(values):
    seq_count, tokens, width = values.shape
    rows = lax.axis_size("row")
    parts = values.reshape(rows, seq_count * tokens // rows, width)
    moved = lax.all_to_all(parts, "row", split_axis=0, concat_axis=0)
    return moved.transpose(1, 0, 2).reshape(parts.shape[1], rows * width)


def from_owner(values, seq_count):
    tokens, width = values.shape
    rows = lax.axis_size("row")
    parts = values.reshape(tokens, rows, width // rows).transpose(1, 0, 2)
    moved = lax.all_to_all(parts, "row", split_axis=0, concat_axis=0)
    return moved.reshape(seq_count, rows * tokens // seq_count, width // rows)


def mm(left_side, right_side):
    return jnp.dot(left_side, right_side, preferred_element_type=jnp.float32)


def mm_nt(left_side, right_side):
    return lax.dot_general(
        left_side, right_side, (((1,), (1,)), ((), ())), preferred_element_type=jnp.float32
    )


def mm_tn(left_side, right_side):
    return lax.dot_general(
        left_side, right_side, (((0,), (0,)), ((), ())), preferred_element_type=jnp.float32
    )


def rms(values):
    factor = lax.rsqrt(jnp.mean(values * values, axis=-1, keepdims=True) + EPSILON)
    return values * factor, factor


def rms_back(grad_values, normed, factor, gain_vec):
    grad_normed = grad_values * gain_vec
    inner = jnp.mean(grad_normed * normed, axis=-1, keepdims=True)
    return (
        factor * (grad_normed - normed * inner),
        jnp.sum(grad_values * normed, axis=0, keepdims=True),
    )


def gather_rows(values, axis):
    return lax.all_gather(values, "row", axis=axis, tiled=True)


def scatter_rows(values, axis):
    return lax.psum_scatter(
        values.astype(jnp.bfloat16), "row", scatter_dimension=axis, tiled=True
    ).astype(jnp.float32)


def both_cores(values, axis):
    return lax.all_gather(values, "seq", axis=axis, tiled=True)


def remote(src, dst, send_sem, recv_sem, device):
    return pltpu.make_async_remote_copy(
        src_ref=src,
        dst_ref=dst,
        send_sem=send_sem,
        recv_sem=recv_sem,
        device_id=device,
        device_id_type=MESH,
    )


def greet(core, row, col):
    barrier = pltpu.get_barrier_semaphore()
    near = [(core, row ^ 1, col), (core, row ^ 2, col), (core, row ^ 3, col), (1 - core, row, col)]
    for device in near:
        pl.semaphore_signal(barrier, inc=1, device_id=device, device_id_type=MESH)

    @pl.when(col > 0)
    def _():
        pl.semaphore_signal(barrier, inc=1, device_id=(core, row, col - 1), device_id_type=MESH)

    @pl.when(col < 3)
    def _():
        pl.semaphore_signal(barrier, inc=1, device_id=(core, row, col + 1), device_id_type=MESH)

    ends = jnp.where((col == 0) | (col == 3), 1, 2)
    pl.semaphore_wait(barrier, 4 + ends)


class Gather:
    def __init__(self, place, buf, rows, sems):
        self.core, self.row, self.col = place
        self.buf, self.rows = buf, rows
        self.send_z, self.recv_z, self.send_s, self.recv_s = sems

    def part(self, core, col, piece):
        rows = self.rows // PIECES
        first = (core * 4 + col) * self.rows + piece * rows
        return self.buf.at[pl.ds(pl.multiple_of(first, rows), rows)]

    def hop(self, dist, right, piece):
        part = self.part(self.core, self.col - dist if right else self.col + dist, piece)
        lane = ((0 if right else 3) + dist) * PIECES + piece
        return remote(
            part,
            part,
            self.send_z.at[lane],
            self.recv_z.at[lane],
            (self.core, self.row, self.col + (1 if right else -1)),
        )

    def came(self, dist, right, piece):
        part = self.part(self.core, self.col - dist if right else self.col + dist, piece)
        lane = ((0 if right else 3) + dist - 1) * PIECES + piece
        return remote(
            part, part, self.send_z.at[lane], self.recv_z.at[lane], (self.core, self.row, self.col)
        )

    def to_sibling(self, col, piece, core=None):
        part = self.part(self.core if core is None else core, col, piece)
        lane = col * PIECES + piece
        return remote(
            part,
            part,
            self.send_s.at[lane],
            self.recv_s.at[lane],
            (1 - self.core, self.row, self.col),
        )

    def start(self):
        col = self.col
        for piece in range(PIECES):

            @pl.when(col < 3)
            def _():
                self.hop(0, True, piece).start()

            @pl.when(col > 0)
            def _():
                self.hop(0, False, piece).start()

        for piece in range(PIECES):
            self.to_sibling(col, piece).start()

    def forward(self, work=()):
        col = self.col
        work = list(work)
        for dist in (1, 2, 3):
            for piece in range(PIECES):

                @pl.when(col >= dist)
                def _():
                    self.came(dist, True, piece).wait_recv()
                    if dist < 3:

                        @pl.when(col < 3)
                        def _():
                            self.hop(dist, True, piece).start()

                    self.to_sibling(col - dist, piece).start()

                @pl.when(col + dist <= 3)
                def _():
                    self.came(dist, False, piece).wait_recv()
                    if dist < 3:

                        @pl.when(col > 0)
                        def _():
                            self.hop(dist, False, piece).start()

                    self.to_sibling(col + dist, piece).start()

            if work:
                work.pop(0)()

    def finish(self):
        for piece in range(PIECES):
            for col in range(4):
                self.to_sibling(col, piece, 1 - self.core).wait_recv()

    def drain(self):
        for piece in range(PIECES):
            for col in range(4):
                self.to_sibling(col, piece).wait_send()
            for dist in (0, 1, 2):

                @pl.when((self.col < 3) & (self.col >= dist))
                def _():
                    self.hop(dist, True, piece).wait_send()

                @pl.when((self.col > 0) & (self.col + dist <= 3))
                def _():
                    self.hop(dist, False, piece).wait_send()


class Scatter:
    def __init__(self, place, rows, bufs, sems):
        self.core, self.row, self.col = place
        self.rows = rows
        self.give, self.keep, self.got, self.sent, self.left, self.right = bufs
        self.send_z, self.recv_z, self.send_s, self.recv_s = sems

    def sibling(self, dest):
        rows = pl.ds(dest * self.rows, self.rows)
        return remote(
            self.give.at[rows],
            self.got.at[rows],
            self.send_s.at[dest],
            self.recv_s.at[dest],
            (1 - self.core, self.row, self.col),
        )

    def start(self):
        for dest in (3, 0, 2, 1):
            self.sibling(dest).start()

    def piece(self, piece):
        rows = self.rows // PIECES
        return pl.ds(piece * rows, rows)

    def mine(self, dest, piece):
        count = self.rows // PIECES
        rows = pl.ds(dest * self.rows + piece * count, count)
        return self.keep[rows].astype(F32) + self.got[rows].astype(F32)

    def inbox(self, dest, right):
        return self.left.at[dest - 1] if right else self.right.at[dest]

    def hop(self, dest, right, piece):
        lane = ((0 if right else 4) + dest) * PIECES + piece
        return remote(
            self.sent.at[dest, self.piece(piece)],
            self.inbox(dest, right).at[self.piece(piece)],
            self.send_z.at[lane],
            self.recv_z.at[lane],
            (self.core, self.row, self.col + (1 if right else -1)),
        )

    def step(self, col, dest, right, piece):
        rows = self.piece(piece)
        if piece == 0:
            self.sibling(dest).wait_recv()
        total = self.mine(dest, piece)
        if col != (0 if right else 3):
            self.hop(dest, right, piece).wait_recv()
            total = total + self.inbox(dest, right)[rows].astype(F32)
        self.sent[dest, rows] = total.astype(BF)
        self.hop(dest, right, piece).start()

    def steps(self, col):
        if col > 1:
            return [
                [(3 - dest, not right, piece) for dest, right, piece in part]
                for part in self.steps(3 - col)
            ]
        full = lambda dest, right: [(dest, right, piece) for piece in range(PIECES)]
        if col == 0:
            return [full(3, True) + full(2, True), full(1, True)]
        near, far = full(3, True) + full(2, True), full(0, False)
        lag, order = PIECES - 1, []
        for index, item in enumerate(near):
            order.append(item)
            if index + 1 >= lag and far:
                order.append(far.pop(0))
        cut = PIECES + 2
        return [order[:cut], order[cut:] + far]

    def run(self, result, work=()):
        work = list(work)
        for part in range(2):
            for col in range(4):

                @pl.when(self.col == col)
                def _():
                    for dest, right, piece in self.steps(col)[part]:
                        self.step(col, dest, right, piece)

            for call in work[part : part + 1]:
                call()
        for call in work[2:]:
            call()
        for dest in range(4):

            @pl.when(self.col == dest)
            def _():
                self.sibling(dest).wait_recv()
                for piece in range(PIECES):
                    rows = self.piece(piece)
                    total = self.mine(dest, piece)
                    for right in (True, False):
                        if dest != (0 if right else 3):
                            self.hop(dest, right, piece).wait_recv()
                            total = total + self.inbox(dest, right)[rows].astype(F32)
                    result[rows] = total

    def drain(self):
        for dest in range(4):
            self.sibling(dest).wait_send()
        for piece in range(PIECES):
            for dest in (1, 2, 3):

                @pl.when(self.col < dest)
                def _():
                    self.hop(dest, True, piece).wait_send()

                @pl.when(self.col > 3 - dest)
                def _():
                    self.hop(3 - dest, False, piece).wait_send()


class RowGather:
    def __init__(self, place, source, block, halves, sems, ways=(1, 2)):
        self.core, self.row, self.col = place
        self.source, self.block, self.halves = source, block, halves
        self.ways = ways
        self.sems = sems

    def neighbour(self, mask):
        return (self.core, self.row ^ mask, self.col)

    def own(self):
        return pltpu.make_async_copy(self.source, self.block(self.row), self.sems.at[8])

    def first(self, mask, block=None):
        lane = mask - 1
        return remote(
            self.source,
            self.block(self.row) if block is None else block,
            self.sems.at[lane],
            self.sems.at[4 + lane],
            self.neighbour(mask),
        )

    def across(self, index, mask):
        return self.block(index) if len(self.ways) == 1 else self.halves(index)[mask - 1]

    def second(self, mask):
        part = self.across(self.row ^ (3 - mask), mask)
        return remote(
            part, part, self.sems.at[1 + mask], self.sems.at[5 + mask], self.neighbour(mask)
        )

    def start(self):
        self.first(1).start()
        self.first(2).start()
        self.own().start()

    def finish_first(self):
        for mask in (1, 2):
            self.first(mask, self.block(self.row ^ mask)).wait_recv()
            self.first(mask).wait_send()
        self.own().wait()

    def forward(self):
        for mask in (1, 2):
            self.first(mask, self.block(self.row ^ mask)).wait_recv()
            if 3 - mask in self.ways:
                self.second(3 - mask).start()

    def finish(self):
        for mask in self.ways:
            part = self.across(self.row ^ 3, mask)
            remote(
                part, part, self.sems.at[1 + mask], self.sems.at[5 + mask], self.neighbour(mask)
            ).wait_recv()
        self.own().wait()
        for mask in (1, 2):
            self.first(mask).wait_send()
        for mask in self.ways:
            self.second(mask).wait_send()


def by_rows(buf, block_rows):
    half = block_rows // 2

    def block(index):
        return buf.at[pl.ds(pl.multiple_of(index * block_rows, block_rows), block_rows)]

    def halves(index):
        return [
            buf.at[pl.ds(pl.multiple_of(index * block_rows + part * half, half), half)]
            for part in range(2)
        ]

    return block, halves


def by_core_rows(core):
    def split(buf, block_rows):
        own = block_rows // 2

        def piece(index, part, count):
            first = index * block_rows + core * own + part * (own // count)
            return buf.at[pl.ds(pl.multiple_of(first, own // count), own // count)]

        return (
            lambda index: piece(index, 0, 1),
            lambda index: [piece(index, part, 2) for part in range(2)],
        )

    return split


def by_half_cols(part):
    def split(buf, block_cols):
        own, rows = block_cols // 2, buf.shape[0] // 2

        def cols(index):
            return pl.ds(pl.multiple_of(index * block_cols + part * own, own), own)

        return (
            lambda index: buf.at[:, cols(index)],
            lambda index: [buf.at[pl.ds(piece * rows, rows), cols(index)] for piece in range(2)],
        )

    return split


def by_cols(buf, block_cols):
    rows = buf.shape[0] // 2

    def block(index):
        return buf.at[:, pl.ds(pl.multiple_of(index * block_cols, block_cols), block_cols)]

    def halves(index):
        cols = pl.ds(pl.multiple_of(index * block_cols, block_cols), block_cols)
        return [buf.at[pl.ds(part * rows, rows), cols] for part in range(2)]

    return block, halves


def gelu_both(values):
    inner = 0.7978845608028654 * (values + 0.044715 * values * values * values)
    bend = jnp.tanh(inner)
    slope = 0.7978845608028654 * (1.0 + 3.0 * 0.044715 * values * values)
    return 0.5 * values * (1.0 + bend), 0.5 * (1.0 + bend) + 0.5 * values * (1.0 - bend * bend) * slope


def head_parts(raw, gain, cosine, sine):
    factor = lax.rsqrt(jnp.mean(raw * raw, axis=1, keepdims=True) + EPSILON)
    half = raw.shape[1] // 2
    scaled = raw * factor * gain
    first, second = scaled[:, :half], scaled[:, half:]
    return jnp.concatenate([first * cosine - second * sine, second * cosine + first * sine], axis=1)


def forward_kernel(
    x_in,
    g_in,
    gains_in,
    w_query,
    w_key,
    w_value,
    w_out,
    w_gate,
    w_up,
    w_down,
    laurel_left,
    laurel_right,
    per_gate,
    per_proj,
    lengths,
    head_gains,
    x_own,
    g_own,
    gains,
    raw_q,
    raw_kv,
    q_low,
    kv,
    lse,
    top,
    o_low,
    attn_val,
    lr_low,
    ff_val,
    laurels,
    vpg,
    vpp,
    cosine,
    sine,
    start,
    wq_all,
    wkv_all,
    wo_all,
    wg_all,
    wu_all,
    wd_all,
    xg_all,
    fg_all,
    gate_all,
    up_all,
    turned_all,
    w_kv_pair,
    laurel_own,
    gains_pad,
    vq,
    vkv,
    vo,
    vg,
    vu,
    vd,
    xg,
    fg,
    gate,
    up,
    hid,
    turned,
    give,
    keep,
    got,
    sent,
    left,
    right,
    give2,
    keep2,
    got2,
    sent2,
    left2,
    right2,
    half_sum,
    row_sems,
    z_send,
    z_recv,
    s_send,
    s_recv,
    misc_send,
    misc_recv,
    out_sems,
):
    core, row, col = lax.axis_index("seq"), lax.axis_index("row"), lax.axis_index("col")
    place = (core, row, col)
    own_tokens, width = x_own.shape
    block = x_in.shape[2]
    head_dim = head_gains.shape[1]
    tokens = xg.shape[0]
    ff_part = gate.shape[1]
    chunk = 2 * own_tokens
    key_width = w_key.shape[1]
    half = row % 2
    half_block = block // 2
    halves2 = (give2, keep2, got2, sent2, left2, right2)
    greet(core, row, col)

    my_cols = pl.ds(pl.multiple_of(row * block, block), block)

    def hand_over(mask):
        return remote(
            x_in.at[row ^ mask],
            x_own.at[:, my_cols],
            misc_send.at[mask],
            misc_recv.at[mask],
            (core, row ^ mask, col),
        )

    def hand_grad(mask):
        return remote(
            g_in.at[row ^ mask],
            g_own.at[:, my_cols],
            misc_send.at[11 + mask],
            misc_recv.at[11 + mask],
            (core, row ^ mask, col),
        )

    def hand_gains(mask):
        return remote(
            gains_pad,
            gains.at[:, my_cols],
            misc_send.at[3 + mask],
            misc_recv.at[3 + mask],
            (core, row ^ mask, col),
        )

    for mask in (3, 1, 2):
        hand_over(mask).start()
    gains_pad[pl.ds(0, 6)] = gains_in[...]
    gains_pad[pl.ds(6, 2)] = jnp.zeros((2, block), F32)
    for mask in (3, 1, 2):
        hand_gains(mask).start()
    x_own[:, my_cols] = x_in[row]
    g_own[:, my_cols] = g_in[row]
    gains[:, my_cols] = gains_pad[...]

    pair_cols = pl.ds(pl.multiple_of(col % 2 * key_width, key_width), key_width)
    w_kv_own = w_kv_pair.at[:, pair_cols]
    w_kv_own[...] = jnp.where(core == 0, w_key[...].astype(F32), w_value[...].astype(F32)).astype(BF)
    pair = remote(w_kv_own, w_kv_own, misc_send.at[7], misc_recv.at[7], (core, row, col ^ 1))
    pair.start()

    lanes = iter(range(32))

    def rows_of(source, buf, split=by_rows, size=block, ways=(1, 2)):
        block_of, halves_of = split(buf, size)
        return RowGather(place, source, block_of, halves_of, row_sems.at[next(lanes)], ways)

    tile = 256
    core_head = pl.ds(pl.multiple_of(core * head_dim, head_dim), head_dim)

    def core_tile(index):
        return pl.ds(pl.multiple_of(core * ff_part + index * tile, tile), tile)

    get_q = rows_of(w_query.at[:, core_head], vq)
    get_kv = rows_of(w_kv_pair, vkv)
    get_o = rows_of(w_out.at[core_head], vo, by_cols, ways=(2,))
    laurel_own[...] = jnp.where(
        core == 0, laurel_left[...].astype(F32), laurel_right[...].astype(F32)
    ).astype(BF)
    get_laurel = [rows_of(laurel_own, laurels.at[core], by_cols)]
    per_rows, per_cols = per_gate.shape[0] // 2, per_proj.shape[0] // 2
    own_rows = pl.ds(pl.multiple_of(core * per_rows, per_rows), per_rows)
    own_cols = pl.ds(pl.multiple_of(core * per_cols, per_cols), per_cols)
    get_per = [
        rows_of(per_gate.at[own_rows], vpg, by_core_rows(core)),
        rows_of(per_proj.at[own_cols], vpp.at[own_cols], by_cols),
    ]
    tiles = ff_part // tile
    get_gu = [
        [
            rows_of(whole.at[:, core_tile(index)], buf.at[:, pl.ds(index * tile, tile)])
            for whole, buf in ((w_gate, vg), (w_up, vu))
        ]
        for index in range(tiles)
    ]
    half_ff = ff_part // 2
    core_ff = pl.ds(pl.multiple_of(core * ff_part, ff_part), ff_part)
    get_d = [
        rows_of(w_down.at[core_ff, pl.ds(part * (block // 2), block // 2)], vd, by_half_cols(part))
        for part in range(2)
    ]

    def per_parts(which, lane):
        parts = [
            vpg.at[pl.ds(pl.multiple_of(index * block + which * per_rows, per_rows), per_rows)]
            for index in range(4)
        ]
        parts.append(vpp.at[pl.ds(pl.multiple_of(which * per_cols, per_cols), per_cols)])
        return list(enumerate(parts, lane))

    def begin(jobs):
        for job in jobs:
            job.start()

    def push(jobs):
        for job in jobs:
            job.forward()

    def complete(jobs):
        for job in jobs:
            job.finish()

    get_q.start()
    pair.wait_recv()
    get_kv.start()

    for mask in (1, 2, 3):
        remote(
            x_in.at[row],
            x_own.at[:, pl.ds(pl.multiple_of((row ^ mask) * block, block), block)],
            misc_send.at[mask],
            misc_recv.at[mask],
            (core, row, col),
        ).wait_recv()
        remote(
            gains_pad,
            gains.at[:, pl.ds(pl.multiple_of((row ^ mask) * block, block), block)],
            misc_send.at[3 + mask],
            misc_recv.at[3 + mask],
            (core, row, col),
        ).wait_recv()

    def own_norm():
        values = x_own[...].astype(F32)
        factor = lax.rsqrt(jnp.mean(values * values, axis=1, keepdims=True) + EPSILON)
        return values, values * factor * gains[pl.ds(0, 1)]

    mine = pl.ds(pl.multiple_of((core * 4 + col) * own_tokens, own_tokens), own_tokens)
    xg[mine] = own_norm()[1].astype(BF)
    sems = lambda lane: (z_send.at[lane], z_recv.at[lane], s_send.at[lane], s_recv.at[lane])
    gather_x = Gather(place, xg, own_tokens, sems(0))
    gather_x.start()

    def doc_tables():
        token = lax.broadcasted_iota(jnp.int32, (tokens, 1), 0)
        token_place = token // own_tokens * chunk + half * own_tokens + token % own_tokens
        doc_start, doc_end = jnp.zeros((tokens, 1), jnp.int32), 0
        for doc in range(lengths.shape[1]):
            length = lengths[row // 2, doc]
            doc_end = doc_end + length
            doc_start = doc_start + jnp.where(token_place >= doc_end, length, 0)
        start[...] = doc_start
        pair_index = lax.broadcasted_iota(jnp.int32, (1, head_dim // 2), 1).astype(F32)
        frequency = jnp.exp(pair_index * (-2.0 * math.log(ROPE_BASE) / head_dim))
        angles = (token_place - doc_start).astype(F32) * frequency
        sine[...] = angles
        cosine[...] = jnp.cos(angles)

    gather_x.forward(
        [
            doc_tables,
            lambda: (push([get_q, get_kv]), begin([get_o])),
        ]
    )
    gather_x.finish()
    sine[...] = jnp.sin(sine[...])
    complete([get_q, get_kv])

    raw_q[...] = mm(xg[...], vq[...])
    raw_kv[...] = mm(xg[...], vkv[...])
    q_low[...] = head_parts(raw_q[...], head_gains[pl.ds(0, 1)], cosine[...], sine[...]).astype(BF)
    is_key = core == 0
    kv_here = head_parts(
        raw_kv[...],
        jnp.where(is_key, head_gains[pl.ds(1, 1)], 1.0),
        jnp.where(is_key, cosine[...], 1.0),
        jnp.where(is_key, sine[...], 0.0),
    ).astype(BF)

    def kv_part(kind, which):
        return kv.at[kind, pl.ds(pl.multiple_of(which * tokens, tokens), tokens)]

    kv[core, pl.ds(pl.multiple_of(half * tokens, tokens), tokens)] = kv_here
    here = kv_part(core, half)
    to_x = remote(here, here, misc_send.at[8], misc_recv.at[8], (core, row ^ 1, col))
    to_s = remote(here, here, misc_send.at[9], misc_recv.at[9], (1 - core, row, col))
    to_x.start()
    to_s.start()
    push([get_o])
    begin(get_gu[0] + get_laurel + get_gu[1])
    came = kv_part(core, half ^ 1)
    remote(here, came, misc_send.at[8], misc_recv.at[8], (core, row, col)).wait_recv()
    on_s = remote(came, came, misc_send.at[10], misc_recv.at[10], (1 - core, row, col))
    on_s.start()
    other = kv_part(1 - core, half)
    remote(other, other, misc_send.at[9], misc_recv.at[9], (core, row, col)).wait_recv()
    other_came = kv_part(1 - core, half ^ 1)
    remote(other_came, other_came, misc_send.at[10], misc_recv.at[10], (core, row, col)).wait_recv()

    q_rows = 128
    key_token = lax.broadcasted_iota(jnp.int32, (1, 2 * tokens), 1)
    in_half = key_token % tokens
    key_place = in_half // own_tokens * chunk + key_token // tokens * own_tokens + in_half % own_tokens
    top[...] = jnp.full(top.shape, MASK_FILL, F32)

    def attend(step, carry):
        first = pl.multiple_of(step * q_rows, q_rows)
        rows = pl.ds(first, q_rows)
        token = first + lax.broadcasted_iota(jnp.int32, (q_rows, 1), 0)
        q_place = token // own_tokens * chunk + half * own_tokens + token % own_tokens
        allowed = (key_place <= q_place) & (key_place >= start[rows])
        scores = jnp.where(allowed, mm_nt(q_low[rows], kv[0]), MASK_FILL)
        row_top = jnp.max(scores, axis=1, keepdims=True)
        weights = jnp.exp(scores - row_top)
        total = jnp.sum(weights, axis=1, keepdims=True)
        probs = (weights * (1.0 / total)).astype(BF)
        o_low[rows] = mm(probs, kv[1]).astype(BF)
        lse[rows] = row_top + jnp.log(total)
        top[...] = jnp.maximum(top[...], jnp.max(row_top))
        return carry

    lax.fori_loop(0, tokens // q_rows, attend, 0)
    get_o.finish()

    away = pl.multiple_of((1 - core) * 4 * own_tokens, 4 * own_tokens)
    home = pl.multiple_of(core * 4 * own_tokens, 4 * own_tokens)
    scatter = Scatter(place, own_tokens, (give, keep, got, sent, left, right), sems(1))

    def project(source, weights, target, first):
        def step(index, carry):
            cols = pl.ds(pl.multiple_of(index * block, block), block)
            value = mm(source[pl.ds(first, 4 * own_tokens)], weights[:, cols])
            target[:, cols] = value.astype(target.dtype)
            return carry

        lax.fori_loop(0, width // block, step, 0)

    project(o_low, vo, give, away)
    scatter.start()
    project(o_low, vo, keep, home)
    scatter.run(
        attn_val,
        [lambda: (push(get_gu[0]), push(get_laurel)), lambda: begin(get_gu[2])],
    )
    push(get_gu[1])
    begin(get_gu[3])

    complete(get_laurel)
    laurel_here = laurels.at[core]
    laurel_share = remote(
        laurel_here, laurel_here, misc_send.at[22], misc_recv.at[22], (1 - core, row, col)
    )
    laurel_share.start()
    inputs, x_norm = own_norm()
    attn_normed = rms(attn_val[...])[0]
    laurel_there = laurels.at[1 - core]
    remote(
        laurel_there, laurel_there, misc_send.at[22], misc_recv.at[22], (core, row, col)
    ).wait_recv()
    lr_low[...] = mm_nt(xg[mine], laurels[0]).astype(BF)
    lo_normed = rms(mm(lr_low[...], laurels[1]))[0]
    h_two = (
        inputs + attn_normed * gains[pl.ds(1, 1)] + (x_norm + lo_normed * gains[pl.ds(2, 1)])
    ) * ROOT_HALF
    fg[mine] = (rms(h_two)[0] * gains[pl.ds(3, 1)]).astype(BF)
    gather_f = Gather(place, fg, own_tokens, sems(2))
    gather_f.start()
    gather_f.forward(
        [
            lambda: None,
            lambda: push(get_gu[2]),
            lambda: begin(get_d[:1]),
        ]
    )
    gather_f.finish()

    def unit_tile(index):
        complete(get_gu[index])
        cols = pl.ds(index * tile, tile)
        bent, slope = gelu_both(mm(fg[...], vg[:, cols]))
        up_part = mm(fg[...], vu[:, cols])
        gate[:, cols] = (up_part * slope).astype(BF)
        up[:, cols] = bent.astype(BF)
        hid[:, cols] = (bent * up_part).astype(BF)

    for index in range(tiles):
        if index == 1:
            push(get_gu[3])
        if index == 3:
            push(get_d[:1])
            begin(get_d[1:])
        unit_tile(index)
    turned[...] = hid[...].T
    scatter_ff = [
        Scatter(place, own_tokens, tuple(buf.at[part] for buf in halves2), sems(3 + part))
        for part in range(2)
    ]

    def project_half(part, target, first):
        def step(index, carry):
            cols = pl.ds(pl.multiple_of(index * block + part * half_block, half_block), half_block)
            here = pl.ds(pl.multiple_of(index * half_block, half_block), half_block)
            value = mm(hid[pl.ds(first, 4 * own_tokens)], vd[:, cols])
            target[:, here] = value.astype(target.dtype)
            return carry

        lax.fori_loop(0, width // block, step, 0)

    def down_half(part):
        complete(get_d[part : part + 1])
        project_half(part, give2.at[part], away)
        scatter_ff[part].start()
        project_half(part, keep2.at[part], home)

    def spread_half(part):
        for index in range(width // block):
            ff_val[:, pl.ds(index * block + part * half_block, half_block)] = half_sum[
                :, pl.ds(index * half_block, half_block)
            ]

    def late():
        push(get_d[1:])
        begin(get_per)
        for mask in (1, 2, 3):
            hand_grad(mask).start()

    down_half(0)
    scatter_ff[0].run(half_sum, [lambda: None, late])
    spread_half(0)
    down_half(1)
    keep_weights = [
        pltpu.make_async_copy(source, target, out_sems.at[lane])
        for lane, (source, target) in enumerate(
            [
                (vq, wq_all),
                (vkv, wkv_all),
                (vo, wo_all),
                (vg, wg_all),
                (vu, wu_all),
                (vd, wd_all),
                (xg, xg_all),
                (fg, fg_all),
                (gate, gate_all),
                (up, up_all),
            ]
        )
    ]
    for copy in keep_weights:
        copy.start()
    get_turned = rows_of(
        turned.at[pl.ds(0, half_ff)], turned_all.at[pl.ds(0, half_ff)], by_cols, tokens
    )
    rest = pl.ds(half_ff, half_ff)
    keep_rest = pltpu.make_async_copy(
        turned.at[rest],
        turned_all.at[rest, pl.ds(pl.multiple_of(row * tokens, tokens), tokens)],
        out_sems.at[10],
    )
    keep_rest.start()
    scatter_ff[1].run(half_sum, [lambda: (push(get_per), get_turned.start())])
    spread_half(1)
    complete(get_per)
    share = [
        remote(part, part, misc_send.at[lane], misc_recv.at[lane], (1 - core, row, col))
        for lane, part in per_parts(core, 16)
    ]
    for copy in share:
        copy.start()
    for lane, part in per_parts(1 - core, 16):
        remote(part, part, misc_send.at[lane], misc_recv.at[lane], (core, row, col)).wait_recv()
    for copy in share:
        copy.wait_send()
    get_turned.finish_first()
    keep_rest.wait()

    for mask in (1, 2, 3):
        hand_over(mask).wait_send()
        hand_gains(mask).wait_send()
        hand_grad(mask).wait_send()
        remote(
            g_in.at[row],
            g_own.at[:, pl.ds(pl.multiple_of((row ^ mask) * block, block), block)],
            misc_send.at[11 + mask],
            misc_recv.at[11 + mask],
            (core, row, col),
        ).wait_recv()
    gather_x.drain()
    scatter.drain()
    gather_f.drain()
    scatter_ff[0].drain()
    scatter_ff[1].drain()
    laurel_share.wait_send()
    pair.wait_send()
    to_x.wait_send()
    to_s.wait_send()
    on_s.wait_send()
    for copy in keep_weights:
        copy.wait()


def run_forward(x_in, g_in, gains_in, weights_in, lengths, head_gains):
    w_gate, laurel_left, per_gate, per_proj = (weights_in[i] for i in (4, 7, 9, 10))
    block = x_in.shape[2]
    own, width = x_in.shape[1], 4 * block
    tokens, head_dim, ff_part = 8 * own, head_gains.shape[1], w_gate.shape[1] // 2
    rank = laurel_left.shape[0]
    vm = pl.BlockSpec(memory_space=pltpu.VMEM)
    hbm = pl.BlockSpec(memory_space=pl.ANY)
    shape = jax.ShapeDtypeStruct
    weights = [
        (width, head_dim),
        (width, head_dim),
        (head_dim, width),
        (width, ff_part),
        (width, ff_part),
        (ff_part, width),
    ]
    acts = [
        (tokens, width),
        (tokens, width),
        (tokens, ff_part),
        (tokens, ff_part),
    ]
    outs = [
        shape((own, width), BF),
        shape((own, width), BF),
        shape((8, width), F32),
        shape((tokens, head_dim), F32),
        shape((tokens, head_dim), F32),
        shape((tokens, head_dim), BF),
        shape((2, 2 * tokens, head_dim), BF),
        shape((tokens, 1), F32),
        shape((8, 128), F32),
        shape((tokens, head_dim), BF),
        shape((own, width), F32),
        shape((own, rank), BF),
        shape((own, width), F32),
        shape((2, rank, width), BF),
        shape((width, per_gate.shape[1]), BF),
        shape((per_proj.shape[0], width), BF),
        shape((tokens, head_dim // 2), F32),
        shape((tokens, head_dim // 2), F32),
        shape((tokens, 1), jnp.int32),
    ] + [shape(size, BF) for size in weights + acts + [(ff_part, 4 * tokens)]]
    scatter_bufs = [
        pltpu.VMEM((4 * own, width), BF),
        pltpu.VMEM((4 * own, width), F32),
        pltpu.VMEM((4 * own, width), BF),
        pltpu.VMEM((4, own, width), BF),
        pltpu.VMEM((3, own, width), BF),
        pltpu.VMEM((3, own, width), BF),
    ]
    dma = pltpu.SemaphoreType.DMA
    return pl.pallas_call(
        forward_kernel,
        out_shape=outs,
        in_specs=[vm, vm, vm, hbm, vm, vm] + [hbm] * 4 + [vm] * 2
        + [hbm] * 2
        + [pl.BlockSpec(memory_space=pltpu.SMEM), vm],
        out_specs=[vm] * 19 + [hbm] * 11,
        scratch_shapes=[
            pltpu.VMEM((block, head_dim), BF),
            pltpu.VMEM((rank, block), BF),
            pltpu.VMEM((8, block), F32),
        ]
        + [pltpu.VMEM(size, BF) for size in weights + acts]
        + [pltpu.VMEM((tokens, ff_part), BF), pltpu.VMEM((ff_part, tokens), BF)]
        + scatter_bufs
        + [pltpu.VMEM((2,) + buf.shape[:-1] + (width // 2,), buf.dtype) for buf in scatter_bufs]
        + [pltpu.VMEM((own, width // 2), F32)]
        + [
            dma((18, 10)),
            dma((5, 8 * PIECES)),
            dma((5, 8 * PIECES)),
            dma((5, 4 * PIECES)),
            dma((5, 4 * PIECES)),
            dma((24,)),
            dma((24,)),
            dma((11,)),
        ],
        compiler_params=pltpu.CompilerParams(
            collective_id=0, has_side_effects=True, vmem_limit_bytes=VMEM_BYTES
        ),
        cost_estimate=pl.CostEstimate(flops=2 * 10**10, bytes_accessed=5 * 10**7, transcendentals=10**6),
    )(x_in, g_in, gains_in, *weights_in, lengths, head_gains)


class RowScatter:
    def __init__(self, place, halves, came, sems, stage=None):
        self.core, self.row, self.col = place
        self.halves, self.came, self.sems = halves, came, sems
        self.stage = stage

    def send(self, lane, index, half, mask):
        return remote(
            self.halves(index)[half],
            self.came.at[lane],
            self.sems.at[lane],
            self.sems.at[6 + lane],
            (self.core, self.row ^ mask, self.col),
        )

    def lane(self, lane):
        index, half, mask = ((1, 0, 1), (3, 0, 1), (2, 1, 2), (3, 1, 2), (2, 0, 2), (1, 1, 1))[lane]
        return self.send(lane, self.row ^ index, half, mask)

    def start(self, lanes=(1, 3, 0, 2)):
        for lane in lanes:
            self.lane(lane).start()

    def load(self, lane):
        slot = {0: 0, 1: 0, 4: 0, 2: 1, 3: 1, 5: 1}[lane]
        return slot, pltpu.make_async_copy(
            self.came.at[lane], self.stage[0].at[slot], self.stage[1].at[slot]
        )

    def fetch(self, *lanes):
        for lane in lanes:
            self.lane(lane).wait_recv()
            if self.stage is not None:
                self.load(lane)[1].start()

    def add(self, lane, index, half):
        if self.stage is None:
            value = self.came[lane]
        else:
            slot, copy = self.load(lane)
            copy.wait()
            value = self.stage[0][slot]
        part = self.halves(self.row ^ index)[half]
        part[...] = (part[...].astype(F32) + value.astype(F32)).astype(BF)

    def middle(self):
        for lane, out, index, half in ((1, 4, 2, 0), (3, 5, 1, 1)):
            self.add(lane, index, half)
            self.lane(out).start()

    def early(self):
        self.add(0, 0, 0)
        self.add(2, 0, 1)

    def finish(self):
        self.add(4, 0, 0)
        self.add(5, 0, 1)

    def drain(self):
        for lane in range(6):
            self.lane(lane).wait_send()


def head_back(grad, raw, gain, cosine, sine):
    factor = lax.rsqrt(jnp.mean(raw * raw, axis=1, keepdims=True) + EPSILON)
    half = raw.shape[1] // 2
    normed = raw * factor
    first, second = grad[:, :half], grad[:, half:]
    back = jnp.concatenate([first * cosine + second * sine, second * cosine - first * sine], axis=1)
    gain_grad = jnp.sum(back * normed, axis=0, keepdims=True)
    inner = back * gain
    return factor * (inner - normed * jnp.mean(inner * normed, axis=1, keepdims=True)), gain_grad


def backward_kernel(
    x_own,
    g_own,
    per_in,
    gains,
    head_gains,
    attn_val,
    lr_low,
    ff_val,
    raw_q,
    raw_kv,
    q_low,
    kv,
    lse,
    top,
    o_low,
    cosine,
    sine,
    start,
    laurels,
    vpg,
    vpp,
    xg_in,
    fg_in,
    gate_in,
    up_in,
    turned_in,
    wq_in,
    wkv_in,
    wo_in,
    wg_in,
    wu_in,
    wd_in,
    y_out,
    x_grad,
    g_gain,
    tops,
    small_a,
    gq,
    gkv,
    gout,
    ggate,
    gup,
    gdown,
    came_g,
    came_u,
    turned_far,
    turned_near,
    vq,
    vkv,
    vo,
    vg,
    vu,
    vd,
    fg,
    gate,
    up,
    dff_all,
    down_stage,
    dffg,
    dattng,
    dgate,
    dup,
    give,
    keep,
    got,
    sent,
    left,
    right,
    own_sum,
    h_two_ref,
    d_three_ref,
    low_ref,
    gpart,
    gcame,
    gpart2,
    gcame2,
    small_give,
    small_keep,
    small_got,
    small_row,
    small_z,
    d_o,
    d_kv,
    kv_give,
    kv_got,
    kv_x_got,
    kv_p_got,
    pkv,
    came_q,
    came_kv,
    came_o,
    stage_g,
    stage_sems,
    load_sems,
    row_sems,
    z_send,
    z_recv,
    s_send,
    s_recv,
    misc_send,
    misc_recv,
    gain_send,
    gain_recv,
    done_sems,
    ff_sems,
    down_sems,
    turned_sems,
    kv_sems,
):
    core, row, col = lax.axis_index("seq"), lax.axis_index("row"), lax.axis_index("col")
    place = (core, row, col)
    own_tokens, width = x_own.shape
    block = width // 4
    tokens, head_dim = raw_q.shape
    ff_part = gate.shape[1]
    chunk = 2 * own_tokens
    key_width = head_dim // 2
    half = row % 2
    rank = lr_low.shape[1]
    my_cols = pl.ds(pl.multiple_of(row * block, block), block)
    mine = pl.ds(pl.multiple_of((core * 4 + col) * own_tokens, own_tokens), own_tokens)
    away = pl.multiple_of((1 - core) * 4 * own_tokens, 4 * own_tokens)
    home = pl.multiple_of(core * 4 * own_tokens, 4 * own_tokens)

    barrier = pltpu.get_barrier_semaphore()
    for mask in (1, 2, 3):
        pl.semaphore_signal(barrier, inc=1, device_id=(core, row ^ mask, col), device_id_type=MESH)
        for other in (0, 1):
            pl.semaphore_signal(
                barrier, inc=1, device_id=(core ^ other, row, col ^ mask), device_id_type=MESH
            )
    pl.semaphore_signal(barrier, inc=1, device_id=(1 - core, row, col), device_id_type=MESH)
    loads = [
        pltpu.make_async_copy(source, target, load_sems.at[lane])
        for lane, (source, target) in enumerate(
            [
                (wd_in, vd),
                (gate_in, gate),
                (up_in, up),
                (wg_in, vg),
                (wu_in, vu),
                (fg_in, fg),
                (wo_in, vo),
                (wq_in, vq),
                (wkv_in, vkv),
            ]
        )
    ]
    for load in loads:
        load.start()
    pl.semaphore_wait(barrier, 10)
    half_ff = ff_part // 2

    def turned_on(part, mask):
        rows = pl.ds(part * half_ff + (mask - 1) * (half_ff // 2), half_ff // 2)
        first = pl.multiple_of((row ^ (3 - mask)) * tokens, tokens)
        if part == 0:
            source = turned_in.at[rows, pl.ds(first, tokens)]
        else:
            source = turned_near.at[2 - mask, pl.ds((mask - 1) * (half_ff // 2), half_ff // 2)]
        lane = part * 2 + mask - 1
        return remote(
            source,
            turned_far.at[rows],
            row_sems.at[0, lane],
            row_sems.at[0, 6 + lane],
            (core, row ^ mask, col),
        )

    def turned_over(mask):
        return remote(
            turned_in.at[
                pl.ds(half_ff, half_ff), pl.ds(pl.multiple_of(row * tokens, tokens), tokens)
            ],
            turned_near.at[mask - 1],
            row_sems.at[0, 3 + mask],
            row_sems.at[0, 9 + mask],
            (core, row ^ mask, col),
        )

    for mask in (1, 2):
        turned_on(0, mask).start()
        turned_over(mask).start()

    def turned_rest():
        for mask in (1, 2):
            turned_over(mask).wait_recv()
        for mask in (1, 2):
            turned_on(1, mask).start()


    def gain(index):
        return gains[pl.ds(index, 1)]

    inputs = x_own[...].astype(F32)
    x_norm = rms(inputs)[0] * gain(0)
    attn_normed = rms(attn_val[...])[0]
    lo_normed = rms(mm(lr_low[...], laurels[1]))[0]
    h_two = (inputs + attn_normed * gain(1) + (x_norm + lo_normed * gain(2))) * ROOT_HALF
    h_two_ref[...] = h_two
    ff_normed, ff_factor = rms(ff_val[...])
    h_three = h_two + ff_normed * gain(4)
    h_low = h_three.astype(BF)
    p_gate, p_proj = vpg[...], vpp[...]
    pg_gelu, pg_slope = gelu_both(mm(h_low, p_gate))
    per_input = per_in[row].astype(F32)
    gp_low = (pg_gelu * per_input).astype(BF)
    pp_normed, pp_factor = rms(mm(gp_low, p_proj))
    low_ref[...] = (h_three + pp_normed * gain(5)).astype(BF)

    def hand_back(source, target, mask, lane):
        return remote(
            source.at[:, pl.ds(pl.multiple_of((row ^ mask) * block, block), block)],
            target.at[row],
            misc_send.at[lane + mask],
            misc_recv.at[lane + mask],
            (core, row ^ mask, col),
        )

    def came_back(target, mask, lane):
        return remote(
            target.at[row ^ mask],
            target.at[row ^ mask],
            misc_send.at[lane + mask],
            misc_recv.at[lane + mask],
            (core, row, col),
        )

    for mask in (1, 2, 3):
        hand_back(low_ref, y_out, mask, 0).start()
    y_out[row] = low_ref[:, my_cols]

    grad_top = g_own[...].astype(F32)
    d_pp, gain_five = rms_back(grad_top, pp_normed, pp_factor, gain(5))
    d_pp_low = d_pp.astype(BF)
    d_pg_low = (mm_nt(d_pp_low, p_proj) * per_input * pg_slope).astype(BF)
    d_three = grad_top + mm_nt(d_pg_low, p_gate)
    d_three_ref[...] = d_three
    d_ff, gain_four = rms_back(d_three, ff_normed, ff_factor, gain(4))
    gpart[...] = jnp.zeros(gpart.shape, F32)
    gpart[pl.ds(5, 1)] = gain_five
    gpart[pl.ds(4, 1)] = gain_four
    dffg[mine] = d_ff.astype(BF)
    sems = lambda lane: (z_send.at[lane], z_recv.at[lane], s_send.at[lane], s_recv.at[lane])
    gather_ff = Gather(place, dffg, own_tokens, sems(0))
    gather_ff.start()

    def small(kind, first, value):
        rows = pl.ds(first, value.shape[0])
        value = value.astype(BF)

        @pl.when(core == kind)
        def _():
            small_keep[rows] = value

        @pl.when(core != kind)
        def _():
            small_give[rows] = value

    small(0, rank, mm_tn(gp_low, d_pp_low))
    small(1, rank, mm_tn(d_pg_low, h_low))
    gather_ff.forward([lambda: None, turned_rest])
    gather_ff.finish()

    part_rows = tokens // 2

    def ff_piece(group, which):
        return dff_all.at[
            pl.ds(pl.multiple_of(group * tokens + which * part_rows, part_rows), part_rows)
        ]

    def ff_over(mask):
        return remote(
            dffg.at[
                pl.ds(pl.multiple_of(core * part_rows, part_rows), part_rows),
                pl.ds(pl.multiple_of((row ^ mask) * block, block), block),
            ],
            ff_piece(row, core),
            ff_sems.at[mask],
            ff_sems.at[4 + mask],
            (core, row ^ mask, col),
        )

    def ff_came(mask):
        part = ff_piece(row ^ mask, core)
        return remote(part, part, ff_sems.at[mask], ff_sems.at[4 + mask], (core, row, col))

    def ff_share(mask, which):
        part = ff_piece(row ^ mask, which)
        return remote(
            part, part, ff_sems.at[8 + mask], ff_sems.at[12 + mask], (1 - core, row, col)
        )

    for mask in (1, 2, 3):
        ff_over(mask).start()
    dff_all[pl.ds(pl.multiple_of(row * tokens, tokens), tokens)] = dffg[:, my_cols]

    tile = 256
    for load in loads[:3]:
        load.wait()

    def units(index, carry):
        cols = pl.ds(pl.multiple_of(index * tile, tile), tile)
        d_hid = mm_nt(dffg[...], vd[cols])
        dgate[:, cols] = (d_hid * gate[:, cols].astype(F32)).astype(BF)
        dup[:, cols] = (d_hid * up[:, cols].astype(F32)).astype(BF)
        return carry

    lax.fori_loop(0, ff_part // tile, units, 0)
    for load in loads[3:5]:
        load.wait()

    def back_ff(target, first):
        rows = pl.ds(first, 4 * own_tokens)

        def step(index, carry):
            cols = pl.ds(pl.multiple_of(index * block, block), block)
            value = mm_nt(dgate[rows], vg[cols]) + mm_nt(dup[rows], vu[cols])
            target[:, cols] = value.astype(target.dtype)
            return carry

        lax.fori_loop(0, width // block, step, 0)

    scatter_f = Scatter(place, own_tokens, (give, keep, got, sent, left, right), sems(1))
    back_ff(give, away)
    scatter_f.start()
    back_ff(keep, home)

    put_g = RowScatter(place, by_rows(vg, block)[1], came_g, row_sems.at[1], (stage_g, stage_sems))
    put_u = RowScatter(place, by_rows(vu, block)[1], came_u, row_sems.at[2], (stage_g, stage_sems))

    def load_turned(lane):
        mask, part = ((0, None), (3, None), (1, 0), (1, 1), (2, 0), (2, 1))[lane]
        cols = pl.ds(pl.multiple_of((row ^ mask) * tokens, tokens), tokens)
        if part is None:
            source = turned_far if mask else turned_in.at[:, cols]
            target = vd.at[:, cols]
        else:
            rows = pl.ds(part * half_ff, half_ff)
            source = turned_near.at[mask - 1] if part else turned_in.at[rows, cols]
            target = vd.at[rows, cols]
        return pltpu.make_async_copy(source, target, turned_sems.at[lane])

    def down_ready():
        for mask in (1, 2):
            for part in range(2):
                turned_on(part, mask).wait_recv()
        for lane in range(6):
            load_turned(lane).start()
        for mask in (1, 2, 3):
            ff_came(mask).wait_recv()
            ff_share(mask, core).start()

    def down_tile(index):
        slot = index % 2
        rows = pl.ds(index * tile, tile)
        target = gdown.at[pl.ds(pl.multiple_of(core * ff_part + index * tile, tile), tile)]
        local = pltpu.make_async_copy(down_stage.at[slot], target, down_sems.at[index])
        over = remote(
            down_stage.at[slot],
            target,
            down_sems.at[4 + index],
            down_sems.at[8 + index],
            (1 - core, row, col),
        )
        return slot, rows, local, over

    def down_grad():
        for lane in range(6):
            load_turned(lane).wait()
        for mask in (1, 2, 3):
            ff_share(mask, 1 - core).wait_recv()
        for index in range(ff_part // tile):
            slot, rows, local, over = down_tile(index)
            if index >= 2:
                before = down_tile(index - 2)
                before[2].wait()
                before[3].wait_send()
            down_stage[slot] = mm(vd[rows], dff_all[...]).astype(BF)
            local.start()
            over.start()

    def gate_grad(target, grad, put):
        def step(index, carry):
            rows = pl.ds(pl.multiple_of(index * tile, tile), tile)
            target[rows] = mm_tn(fg[:, rows], grad[...]).astype(BF)
            return carry

        lax.fori_loop(0, width // tile, step, 0)

    def start_gate():
        loads[5].wait()
        gate_grad(vg, dgate, put_g)
        put_g.start()

    def start_up():
        gate_grad(vu, dup, put_u)
        put_u.start((1, 3))

    start_gate()
    scatter_f.run(own_sum, [start_up, down_ready])

    gather_ff.drain()
    f_normed, f_factor = rms(h_two_ref[...])
    d_f, gain_three = rms_back(own_sum[...], f_normed, f_factor, gain(3))
    d_half = (d_three_ref[...] + d_f) * ROOT_HALF
    d_three_ref[...] = d_half
    attn_normed, attn_factor = rms(attn_val[...])
    d_attn, gain_one = rms_back(d_half, attn_normed, attn_factor, gain(1))
    dattng[mine] = d_attn.astype(BF)
    gather_a = Gather(place, dattng, own_tokens, sems(2))
    gather_a.start()
    lo_normed, lo_factor = rms(mm(lr_low[...], laurels[1]))
    d_lo, gain_two = rms_back(d_half, lo_normed, lo_factor, gain(2))
    d_lo_low = d_lo.astype(BF)
    d_lr_low = mm_nt(d_lo_low, laurels[1]).astype(BF)
    small(0, 0, mm_tn(lr_low[...], d_lo_low))
    x_low = (rms(x_own[...].astype(F32))[0] * gain(0)).astype(BF)
    small(1, 0, mm_tn(d_lr_low, x_low))
    own_sum[...] = d_half + mm(d_lr_low, laurels[0])
    gpart[pl.ds(3, 1)] = gain_three
    gpart[pl.ds(2, 1)] = gain_two
    gpart[pl.ds(1, 1)] = gain_one
    small_swap = remote(
        small_give, small_got, misc_send.at[8], misc_recv.at[8], (1 - core, row, col)
    )
    small_swap.start()
    put_s = RowScatter(place, by_cols(small_keep, block)[1], small_row, row_sems.at[6])

    def small_sum():
        small_swap.wait_recv()
        small_keep[...] = (small_keep[...].astype(F32) + small_got[...].astype(F32)).astype(BF)

    def middle_gate():
        put_g.fetch(1, 3)
        down_grad()
        put_g.middle()

    def more_small():
        small_sum()
        put_g.fetch(0, 2)

    gather_a.forward([middle_gate, more_small, put_g.early])
    gather_a.finish()
    scatter_f.drain()

    loads[6].wait()
    d_o[...] = mm_nt(dattng[...], vo[...]).astype(BF)
    q_rows = 128
    key_token = lax.broadcasted_iota(jnp.int32, (1, 2 * tokens), 1)
    in_half = key_token % tokens
    key_place = in_half // own_tokens * chunk + key_token // tokens * own_tokens + in_half % own_tokens
    d_kv[...] = jnp.zeros(d_kv.shape, F32)

    def attend(step, carry):
        first = pl.multiple_of(step * q_rows, q_rows)
        rows = pl.ds(first, q_rows)
        token = first + lax.broadcasted_iota(jnp.int32, (q_rows, 1), 0)
        q_place = token // own_tokens * chunk + half * own_tokens + token % own_tokens
        allowed = (key_place <= q_place) & (key_place >= start[rows])
        scores = jnp.where(allowed, mm_nt(q_low[rows], kv[0]), MASK_FILL)
        probs = jnp.exp(scores - lse[rows])
        d_probs = mm_nt(d_o[rows], kv[1])
        delta = jnp.sum(probs * d_probs, axis=1, keepdims=True)
        d_scores = (probs * (d_probs - delta)).astype(BF)
        d_kv[0] += mm_tn(d_scores, q_low[rows])
        d_kv[1] += mm_tn(probs.astype(BF), d_o[rows])
        d_raw, gain_part = head_back(
            mm(d_scores, kv[0]), raw_q[rows], head_gains[pl.ds(0, 1)], cosine[rows], sine[rows]
        )
        d_o[rows] = d_raw.astype(BF)
        return carry + gain_part

    gain_q = lax.fori_loop(0, tokens // q_rows, attend, jnp.zeros((1, head_dim), F32))

    kv_give[...] = d_kv[1 - core].astype(BF)
    swap_kv = remote(kv_give, kv_got, misc_send.at[9], misc_recv.at[9], (1 - core, row, col))
    swap_kv.start()

    def out_grad():
        for part in range(2):
            wide = pl.ds(part * (width // 2), width // 2)
            vo[:, wide] = mm_tn(o_low[...], dattng[:, wide]).astype(BF)

    put_o = RowScatter(place, by_cols(vo, block)[1], came_o, row_sems.at[3])
    swap_kv.wait()
    kv_x = kv_give.at[pl.ds(0, tokens)]
    theirs = pl.ds(pl.multiple_of((half ^ 1) * tokens, tokens), tokens)
    ours = pl.ds(pl.multiple_of(half * tokens, tokens), tokens)
    kv_x[...] = (d_kv[core, theirs] + kv_got[theirs].astype(F32)).astype(BF)
    kv_half = tokens // 2

    def over_x(piece):
        rows = pl.ds(piece * kv_half, kv_half)
        return remote(
            kv_x.at[rows],
            kv_x_got.at[rows],
            kv_sems.at[piece],
            kv_sems.at[2 + piece],
            (core, row ^ 1, col),
        )

    def over_p(piece):
        rows = pl.ds(piece * kv_half, kv_half)
        return remote(
            kv_p.at[rows],
            kv_p_got.at[rows],
            kv_sems.at[4 + piece],
            kv_sems.at[6 + piece],
            (core, row, col ^ 1),
        )

    for piece in range(2):
        over_x(piece).start()
    put_u.start((0, 2))
    load_x = pltpu.make_async_copy(xg_in, dffg, load_sems.at[10])
    for mask in (1, 2, 3):
        ff_over(mask).wait_send()
    load_x.start()
    put_u.fetch(1, 3)
    out_grad()
    put_u.middle()
    put_s.start()
    put_o.start()
    loads[7].wait()
    loads[8].wait()
    kv_p = kv_got.at[pl.ds(0, tokens)]
    d_kind = d_kv[core, ours] + kv_got[ours].astype(F32)
    for piece in range(2):
        rows = pl.ds(piece * kv_half, kv_half)
        over_x(piece).wait_recv()
        part = d_kind[piece * kv_half : (piece + 1) * kv_half] + kv_x_got[rows].astype(F32)
        kv_p[rows] = part.astype(BF)
        over_p(piece).start()
    for piece in range(2):
        over_p(piece).wait()
    d_kind = kv_p[...].astype(F32) + kv_p_got[...].astype(F32)
    is_key = core == 0
    d_kind_raw, gain_k = head_back(
        d_kind,
        raw_kv[...],
        jnp.where(is_key, head_gains[pl.ds(1, 1)], 1.0),
        jnp.where(is_key, cosine[...], 1.0),
        jnp.where(is_key, sine[...], 0.0),
    )
    for part in range(4):
        gpart[pl.ds(6, 1), pl.ds(part * block, head_dim)] = gain_q
        gpart[pl.ds(6, 1), pl.ds(part * block + head_dim, head_dim)] = gain_k * jnp.where(
            is_key, 0.5, 0.0
        )
    kv_p[...] = d_kind_raw.astype(BF)
    pair_cols = pl.ds(pl.multiple_of(col % 2 * key_width, key_width), key_width)

    def back_heads(target, first):
        rows = pl.ds(first, 4 * own_tokens)

        def step(index, carry):
            cols = pl.ds(pl.multiple_of(index * block, block), block)
            value = mm_nt(d_o[rows], vq[cols]) + mm_nt(kv_p[rows, pair_cols], vkv[cols, pair_cols])
            target[:, cols] = value.astype(target.dtype)
            return carry

        lax.fori_loop(0, width // block, step, 0)

    scatter_x = Scatter(place, own_tokens, (give, keep, got, sent, left, right), sems(3))
    back_heads(give, away)
    scatter_x.start()
    back_heads(keep, home)
    put_q = RowScatter(place, by_rows(vq, block)[1], came_q, row_sems.at[4])
    put_kv = RowScatter(place, by_rows(pkv, block)[1], came_kv, row_sems.at[5])

    def query_grad():
        load_x.wait()

        def step(index, carry):
            rows = pl.ds(pl.multiple_of(index * tile, tile), tile)
            vq[rows] = mm_tn(dffg[:, rows], d_o[...]).astype(BF)
            pkv[rows] = mm_tn(dffg[:, rows], kv_p[:, pair_cols]).astype(BF)
            return carry

        lax.fori_loop(0, width // tile, step, 0)
        put_q.start()
        put_kv.start()

    def deliver(lane, source, target):
        local = pltpu.make_async_copy(source, target, done_sems.at[lane])
        over = remote(
            source, target, done_sems.at[8 + lane], done_sems.at[16 + lane], (1 - core, row, col)
        )
        local.start()
        over.start()
        done.append((local, over))

    core_ff = pl.ds(pl.multiple_of(core * ff_part, ff_part), ff_part)
    core_head = pl.ds(pl.multiple_of(core * head_dim, head_dim), head_dim)
    sib_ff = pl.ds(pl.multiple_of((1 - core) * ff_part, ff_part), ff_part)
    sib_head = pl.ds(pl.multiple_of((1 - core) * head_dim, head_dim), head_dim)
    row_block = pl.ds(pl.multiple_of(row * block, block), block)
    done = []

    quarter = block // 4

    def small_quarter(mask):
        return remote(
            small_keep.at[
                :, pl.ds(pl.multiple_of(row * block + (col ^ mask) * quarter, quarter), quarter)
            ],
            small_z.at[mask],
            misc_send.at[11 + mask],
            misc_recv.at[11 + mask],
            (core, row, col ^ mask),
        )

    def gate_finish():
        put_g.fetch(4, 5)
        put_g.finish()
        deliver(1, vg.at[row_block], ggate.at[:, core_ff])
        put_u.fetch(0, 2)
        put_u.early()

    d_half_here = d_three_ref
    scatter_x.run(h_two_ref, [query_grad, gate_finish])
    d_xn = own_sum[...] + h_two_ref[...]
    x_normed, x_factor = rms(x_own[...].astype(F32))
    d_in, gain_zero = rms_back(d_xn, x_normed, x_factor, gain(0))
    gpart[pl.ds(0, 1)] = gain_zero
    for mask in (1, 2, 3):
        hand_back(low_ref, y_out, mask, 0).wait_send()
    low_ref[...] = (d_half_here[...] + d_in).astype(BF)
    for mask in (1, 2, 3):
        hand_back(low_ref, x_grad, mask, 4).start()
    x_grad[row] = low_ref[:, my_cols]

    gpart[pl.ds(8, 8)] = jnp.full((8, width), jnp.max(top[...]), F32)

    def gain_row(mask):
        return remote(
            gpart.at[:, pl.ds(pl.multiple_of((row ^ mask) * block, block), block)],
            gcame.at[mask],
            gain_send.at[mask],
            gain_recv.at[mask],
            (core, row ^ mask, col),
        )

    for mask in (1, 2, 3):
        gain_row(mask).start()
    gcame[0] = gpart[:, my_cols]
    for put in (put_s, put_o, put_q, put_kv):
        put.fetch(1, 3)
        put.middle()
    for mask in (1, 2, 3):
        gain_row(mask).wait_recv()
    summed = gcame[0] + gcame[1] + gcame[2] + gcame[3]
    largest = jnp.maximum(jnp.maximum(gcame[0], gcame[1]), jnp.maximum(gcame[2], gcame[3]))
    gpart2[pl.ds(0, 8)] = summed[:8]
    gpart2[pl.ds(8, 8)] = largest[8:]
    me = core * 4 + col
    members = [(other, mask) for other in (0, 1) for mask in range(4) if other or mask]

    def gain_group(other, mask):
        lane = 4 + other * 4 + mask
        return remote(
            gpart2,
            gcame2.at[me],
            gain_send.at[lane],
            gain_recv.at[lane],
            (core ^ other, row, col ^ mask),
        )

    for other, mask in members:
        gain_group(other, mask).start()
    gcame2[me] = gpart2[...]
    put_s.fetch(0, 2, 4, 5)
    put_s.early()
    put_s.finish()
    for mask in (1, 2, 3):
        small_quarter(mask).start()
    put_u.fetch(4, 5)
    put_u.finish()
    deliver(2, vu.at[row_block], gup.at[:, core_ff])

    def small_share(other, mask):
        lane = 16 + other * 4 + mask
        return remote(
            kv_x.at[pl.ds(0, small_keep.shape[0]), pl.ds(0, quarter)],
            small_a.at[core, col],
            misc_send.at[lane],
            misc_recv.at[lane],
            (core ^ other, row, col ^ mask),
        )

    for mask in (1, 2, 3):
        small_quarter(mask).wait_recv()
    small_total = small_keep[
        :, pl.ds(pl.multiple_of(row * block + col * quarter, quarter), quarter)
    ].astype(F32)
    for mask in (1, 2, 3):
        small_total = small_total + small_z[mask].astype(F32)
    for piece in range(2):
        over_x(piece).wait_send()
    kv_x[pl.ds(0, small_keep.shape[0]), pl.ds(0, quarter)] = small_total.astype(BF)
    for other, mask in members:
        small_share(other, mask).start()
    small_a[core, col] = small_total.astype(BF)
    for put, lane, source, target in (
        (put_o, 4, vo.at[:, row_block], gout.at[core_head]),
        (put_kv, 3, pkv.at[row_block], gkv.at[core]),
        (put_q, 5, vq.at[row_block], gq.at[:, core_head]),
    ):
        put.fetch(0, 2, 4, 5)
        put.early()
        put.finish()
        deliver(lane, source, target)

    for other, mask in members:
        who = (core ^ other) * 4 + (col ^ mask)
        lane = 4 + other * 4 + mask
        remote(
            gpart2, gcame2.at[who], gain_send.at[lane], gain_recv.at[lane], (core, row, col)
        ).wait_recv()
    total = gcame2[0]
    for who in range(1, 8):
        total = total + gcame2[who]
    g_gain[...] = total[:8]
    for who in range(8):
        head = 2 * (who % 4) + who // 4
        tops[pl.ds(head, 1)] = gcame2[who, pl.ds(8, 1), pl.ds(0, 128)]

    gather_a.drain()
    scatter_x.drain()
    for other, mask in members:
        part = small_a.at[core ^ other, col ^ mask]
        lane = 16 + other * 4 + mask
        remote(part, part, misc_send.at[lane], misc_recv.at[lane], (core, row, col)).wait_recv()
        small_share(other, mask).wait_send()
        gain_group(other, mask).wait_send()
    for mask in (1, 2, 3):
        came_back(y_out, mask, 0).wait_recv()
        came_back(x_grad, mask, 4).wait_recv()
        hand_back(low_ref, x_grad, mask, 4).wait_send()
        gain_row(mask).wait_send()
        small_quarter(mask).wait_send()
    small_swap.wait_send()
    for put in (put_g, put_u, put_o, put_q, put_kv, put_s):
        put.drain()
    for mask in (1, 2):
        turned_over(mask).wait_send()
        for part in range(2):
            turned_on(part, mask).wait_send()
    for mask in (1, 2, 3):
        ff_share(mask, core).wait_send()
    for index in range(ff_part // tile):
        slot, rows, local, over = down_tile(index)
        if index >= 2:
            local.wait()
            over.wait_send()
        target = gdown.at[pl.ds(pl.multiple_of((1 - core) * ff_part + index * tile, tile), tile)]
        remote(
            target, target, down_sems.at[4 + index], down_sems.at[8 + index], (core, row, col)
        ).wait_recv()
    theirs_at = {
        1: ggate.at[:, sib_ff],
        2: gup.at[:, sib_ff],
        3: gkv.at[1 - core],
        4: gout.at[sib_head],
        5: gq.at[:, sib_head],
    }
    for lane, (local, over) in zip((1, 2, 4, 3, 5), done):
        local.wait()
        over.wait_send()
        target = theirs_at[lane]
        remote(
            target, target, done_sems.at[8 + lane], done_sems.at[16 + lane], (core, row, col)
        ).wait_recv()


def run_backward(small_args, big_args):
    x_own, per_in, head_gains = small_args[0], small_args[2], small_args[4]
    own, width = x_own.shape
    block = width // 4
    gate = big_args[2]
    tokens, ff_part = gate.shape
    head_dim = head_gains.shape[1]
    rank = small_args[6].shape[1]
    small_rows = small_args[18].shape[1] + small_args[20].shape[0]
    vm = pl.BlockSpec(memory_space=pltpu.VMEM)
    hbm = pl.BlockSpec(memory_space=pl.ANY)
    shape = jax.ShapeDtypeStruct
    vmem = pltpu.VMEM
    dma = pltpu.SemaphoreType.DMA
    outs = [
        shape((4, own, block), BF),
        shape((4, own, block), BF),
        shape((8, block), F32),
        shape((8, 128), F32),
        shape((2, 4, small_rows, block // 4), BF),
        shape((block, 2 * head_dim), BF),
        shape((2, block, head_dim // 2), BF),
        shape((2 * head_dim, block), BF),
        shape((block, 2 * ff_part), BF),
        shape((block, 2 * ff_part), BF),
        shape((2 * ff_part, block), BF),
        shape((6, block // 2, ff_part), BF),
        shape((6, block // 2, ff_part), BF),
        shape((ff_part, tokens), BF),
        shape((2, ff_part // 2, tokens), BF),
    ]
    scratch = [
        vmem((width, head_dim), BF),
        vmem((width, head_dim), BF),
        vmem((head_dim, width), BF),
        vmem((width, ff_part), BF),
        vmem((width, ff_part), BF),
        vmem((ff_part, width), BF),
        vmem((tokens, width), BF),
        vmem((tokens, ff_part), BF),
        vmem((tokens, ff_part), BF),
        vmem((4 * tokens, block), BF),
        vmem((2, 256, block), BF),
        vmem((tokens, width), BF),
        vmem((tokens, width), BF),
        vmem((tokens, ff_part), BF),
        vmem((tokens, ff_part), BF),
        vmem((4 * own, width), BF),
        vmem((4 * own, width), F32),
        vmem((4 * own, width), BF),
        vmem((4, own, width), BF),
        vmem((3, own, width), BF),
        vmem((3, own, width), BF),
        vmem((own, width), F32),
        vmem((own, width), F32),
        vmem((own, width), F32),
        vmem((own, width), BF),
        vmem((16, width), F32),
        vmem((4, 16, block), F32),
        vmem((16, block), F32),
        vmem((8, 16, block), F32),
        vmem((small_rows, width), BF),
        vmem((small_rows, width), BF),
        vmem((small_rows, width), BF),
        vmem((6, small_rows // 2, block), BF),
        vmem((4, small_rows, block // 4), BF),
        vmem((tokens, head_dim), BF),
        vmem((2, 2 * tokens, head_dim), F32),
        vmem((2 * tokens, head_dim), BF),
        vmem((2 * tokens, head_dim), BF),
        vmem((tokens, head_dim), BF),
        vmem((tokens, head_dim), BF),
        vmem((width, head_dim // 2), BF),
        vmem((6, block // 2, head_dim), BF),
        vmem((6, block // 2, head_dim // 2), BF),
        vmem((6, head_dim // 2, block), BF),
        vmem((2, block // 2, ff_part), BF),
        dma((2,)),
        dma((11,)),
        dma((7, 12)),
        dma((4, 8 * PIECES)),
        dma((4, 8 * PIECES)),
        dma((4, 4 * PIECES)),
        dma((4, 4 * PIECES)),
        dma((24,)),
        dma((24,)),
        dma((12,)),
        dma((12,)),
        dma((24,)),
        dma((16,)),
        dma((12,)),
        dma((6,)),
        dma((8,)),
    ]
    return pl.pallas_call(
        backward_kernel,
        out_shape=outs,
        in_specs=[vm] * 21 + [hbm] * 11,
        out_specs=[vm] * 5 + [hbm] * 10,
        scratch_shapes=scratch,
        compiler_params=pltpu.CompilerParams(
            collective_id=1, has_side_effects=True, vmem_limit_bytes=VMEM_BYTES
        ),
        cost_estimate=pl.CostEstimate(
            flops=4 * 10**10, bytes_accessed=10**8, transcendentals=2 * 10**6
        ),
    )(*small_args, *big_args)


def finish_kernel(
    y_in,
    x_in,
    gains,
    tops,
    small,
    gq,
    gkv,
    gout,
    ggate,
    gup,
    gdown,
    head_gains,
    y_out,
    x_out,
    o_query,
    o_key,
    o_value,
    o_out,
    o_gate,
    o_up,
    o_down,
    o_left,
    o_right,
    o_per_gate,
    o_per_proj,
    o_gains,
    o_head,
    o_clip,
):
    o_query[...] = gq[...].astype(F32)
    o_key[...] = gkv[0].astype(F32)
    o_value[...] = gkv[1].astype(F32)
    o_out[...] = gout[...].astype(F32)
    o_gate[...] = ggate[...].astype(F32)
    o_up[...] = gup[...].astype(F32)
    o_down[...] = gdown[...].astype(F32)
    head_dim = head_gains.shape[1]
    quarter = small.shape[3]
    rank = o_right.shape[0]

    @pl.when(pl.program_id(0) == 0)
    def _():
        own = y_in.shape[1]
        for part in range(4):
            rows = pl.ds(part % 2 * own, own)
            y_out[part // 2, rows] = y_in[part]
            x_out[part // 2, rows] = x_in[part]

    @pl.when(pl.program_id(0) == 1)
    def _():
        for part in range(4):
            cols = pl.ds(part * quarter, quarter)
            first = small[0, part].astype(F32)
            o_right[:, cols] = first[:rank]
            o_per_proj[:, cols] = first[rank:]
            second = small[1, part].astype(F32)
            o_left[:, cols] = second[:rank]
            o_per_gate[cols] = second[rank:].T

    @pl.when(pl.program_id(0) == 1)
    def _():
        o_gains[...] = gains[pl.ds(0, 6)]
        o_head[pl.ds(0, 1)] = gains[pl.ds(6, 1), pl.ds(0, head_dim)]
        o_head[pl.ds(1, 1)] = gains[pl.ds(6, 1), pl.ds(head_dim, head_dim)]
        factor = jnp.sqrt(CLIP_LEVEL / jnp.maximum(tops[...], CLIP_LEVEL))[:, :1]
        o_clip[0] = factor * head_gains[pl.ds(0, 1)]
        o_clip[1] = factor * head_gains[pl.ds(1, 1)]


def run_finish(results, head_gains, rank):
    y_out, x_grad, g_gain, tops, small, gq, gkv, gout, ggate, gup, gdown = results
    steps = 2
    shape = jax.ShapeDtypeStruct

    def whole(array):
        dims = len(array.shape)
        return pl.BlockSpec(array.shape, lambda step: (0,) * dims)

    def rows(array):
        size = (array.shape[0] // steps, array.shape[1])
        return pl.BlockSpec(size, lambda step: (step, 0))

    own, block = y_out.shape[1:]
    key_width = gkv.shape[2]
    proj = small.shape[2] - rank
    tokens_shape = shape((2, 2 * own, block), BF)
    by_rows_out = [
        shape(gq.shape, F32),
        shape(gkv.shape[1:], F32),
        shape(gkv.shape[1:], F32),
        shape(gout.shape, F32),
        shape(ggate.shape, F32),
        shape(gup.shape, F32),
        shape(gdown.shape, F32),
    ]
    whole_out = [
        shape((rank, block), F32),
        shape((rank, block), F32),
        shape((block, proj), F32),
        shape((proj, block), F32),
        shape((6, block), F32),
        shape(head_gains.shape, F32),
        shape((2, tops.shape[0], head_gains.shape[1]), F32),
    ]
    kv_spec = pl.BlockSpec((2, block // steps, key_width), lambda step: (0, step, 0))
    return pl.pallas_call(
        finish_kernel,
        grid=(steps,),
        out_shape=[tokens_shape, tokens_shape] + by_rows_out + whole_out,
        in_specs=[whole(y_out), whole(x_grad), whole(g_gain), whole(tops), whole(small), rows(gq), kv_spec]
        + [rows(array) for array in (gout, ggate, gup, gdown)]
        + [whole(head_gains)],
        out_specs=[whole(tokens_shape)] * 2
        + [rows(array) for array in by_rows_out]
        + [whole(array) for array in whole_out],
        compiler_params=pltpu.CompilerParams(vmem_limit_bytes=VMEM_BYTES),
        cost_estimate=pl.CostEstimate(flops=10**7, bytes_accessed=3 * 10**7, transcendentals=0),
    )(*results, head_gains)


def body_pair(
    layer_in,
    per_layer_in,
    doc_lengths,
    w_query,
    w_key,
    w_value,
    w_out,
    w_gate,
    w_up,
    w_down,
    laurel_left,
    laurel_right,
    per_gate,
    per_proj,
    norm_gains,
    head_gains,
    out_grad,
):
    core, row, col = lax.axis_index("seq"), lax.axis_index("row"), lax.axis_index("col")
    rows, cols, cores = lax.axis_size("row"), lax.axis_size("col"), lax.axis_size("seq")
    seq_count = layer_in.shape[0]
    head_dim = head_gains.shape[1]
    key_width = w_key.shape[1]
    ff_part = w_gate.shape[1] // cores
    chunk = layer_in.shape[1]
    halves = rows // seq_count
    own_tokens = chunk // halves
    group_tokens = own_tokens * cores * cols
    even_col = col % 2 == 0

    rank = laurel_left.shape[1]
    saved = run_forward(
        layer_in.reshape(rows, own_tokens, -1),
        out_grad.reshape(rows, own_tokens, -1),
        norm_gains,
        (
            w_query,
            w_key,
            w_value,
            w_out,
            w_gate,
            w_up,
            w_down,
            laurel_left.T,
            laurel_right,
            per_gate,
            per_proj,
        ),
        doc_lengths,
        head_gains,
    )
    (x_own, g_own, gains, raw_q, raw_kv, q_low, kv, lse, top_tile, o_low, attn_val, lr_low, ff_val) = saved[
        :13
    ]
    laurels, p_gate, p_proj, cosine, sine, start = saved[13:19]
    w_q, w_kv_all, w_o, w_g, w_u, w_d, x_all, f_all, gate_val, up_val, turned = saved[19:]
    results = run_backward(
        (
            x_own,
            g_own,
            per_layer_in.reshape(rows, own_tokens, -1),
            gains,
            head_gains,
            attn_val,
            lr_low,
            ff_val,
            raw_q,
            raw_kv,
            q_low,
            kv,
            lse,
            top_tile,
            o_low,
            cosine,
            sine,
            start,
            laurels,
            p_gate,
            p_proj,
        ),
        (x_all, f_all, gate_val, up_val, turned, w_q, w_kv_all, w_o, w_g, w_u, w_d),
    )
    finished = list(run_finish(results[:11], head_gains, rank))
    finished[9] = finished[9].T
    return tuple(finished)


def solution(mesh):
    sizes = tuple(mesh.shape[axis] for axis in ("seq", "row", "col"))
    body = body_pair if sizes == (2, 4, 4) else body_any
    return jax.shard_map(
        body,
        mesh=mesh,
        in_specs=(
            P(None, ("seq", "col"), "row"),
            P(None, ("seq", "col"), None),
            P(),
            P("row", "col"),
            P("row", "col"),
            P("row", "col"),
            P("col", "row"),
            P("row", "col"),
            P("row", "col"),
            P("col", "row"),
            P("row", None),
            P(None, "row"),
            P("row", None),
            P(None, "row"),
            P(None, "row"),
            P(),
            P(None, ("seq", "col"), "row"),
        ),
        out_specs=(
            P(None, ("seq", "col"), "row"),
            P(None, ("seq", "col"), "row"),
            P("row", "col"),
            P("row", "col"),
            P("row", "col"),
            P("col", "row"),
            P("row", "col"),
            P("row", "col"),
            P("col", "row"),
            P("row", None),
            P(None, "row"),
            P("row", None),
            P(None, "row"),
            P(None, "row"),
            P(),
            P(),
        ),
        check_vma=False,
    )
```

profile of v0, /device:TPU:1, one launch (start us, length us, event | category | flops | bytes accessed | tf_op | source)
XLA Modules:
  0.0 367.3 jit_solution(10916161077082097462)
XLA Ops:
  0.7 175.2 %shard_map.288 = (bf16[64,2048]{1,0:T(8,128)(2,1)}, bf16[64,2048]{1,0:T(8,128)(2,1)}, f32[8,2048]{1,0:T(8,128)}, f32[512,256]{1,0:T(8,128)}, f32[512,256]{1,0:T(...) custom-call(bf16[4,64,512]{2,1,0:T(8,128)(2,1)} %bitcast.5, ...), custom_call_target="tpu_custom_call" | custom-call | flops 20000000000 | bytes 50000000 | tf_op jit(solution)/shard_map/pallas_call | solution.py:1404
  175.9 182.1 %shard_map.289 = (bf16[4,64,512]{2,1,0:T(8,128)(2,1)}, bf16[4,64,512]{2,1,0:T(8,128)(2,1)}, f32[8,512]{1,0:T(8,128)}, f32[8,128]{1,0:T(8,128)}, bf16[2,4,320,128...) custom-call(bf16[64,2048]{1,0:T(8,128)(2,1)} %get-tuple-element.73.x, ...), custom_call_target="tpu_custom_call" | custom-call | flops 40000000000 | bytes 100000000 | tf_op jit(solution)/shard_map/pallas_call | solution.py:2383
  358.0 9.0 %shard_map.290 = (bf16[2,128,512]{2,1,0:T(8,128)(2,1)}, bf16[2,128,512]{2,1,0:T(8,128)(2,1)}, f32[512,512]{1,0:T(8,128)}, f32[512,128]{1,0:T(8,128)}, f32[512,12...) custom-call(bf16[4,64,512]{2,1,0:T(8,128)(2,1)} %get-tuple-element.1, ...), custom_call_target="tpu_custom_call" | custom-call | flops 10000000 | bytes 30000000 | tf_op jit(solution)/shard_map/pallas_call | solution.py:2504
where the time goes:
time: 372 us; the launch traced here: 367 us
  Pallas kernels  366 us (98%)
    pallas_call x1, Pallas kernels, run_backward(): pl.pallas_call(backward_kernel, out_shape=outs, in_specs=[vm] * 21 + [hbm...  182 us
    pallas_call x1, Pallas kernels, run_forward(): pl.pallas_call(forward_kernel, out_shape=outs, in_specs=[vm, vm, vm, hbm,...  175 us
    pallas_call x1, Pallas kernels, run_finish(): pl.pallas_call(finish_kernel, grid=(steps,), out_shape=[tokens_shape, tok...  9.02 us

commit v1 on v0

--- a/solution.py
+++ b/solution.py
@@ -17,6 +17,7 @@
 F32 = jnp.float32
 VMEM_BYTES = 63 * 2**20
 PIECES = 4
+TURNED_PART = 4
 
 
 def swapped(value, axis, apart):
@@ -1297,10 +1298,11 @@
     ]
     for copy in keep_weights:
         copy.start()
+    cut = ff_part // TURNED_PART
     get_turned = rows_of(
-        turned.at[pl.ds(0, half_ff)], turned_all.at[pl.ds(0, half_ff)], by_cols, tokens
-    )
-    rest = pl.ds(half_ff, half_ff)
+        turned.at[pl.ds(0, cut)], turned_all.at[pl.ds(0, cut)], by_cols, tokens
+    )
+    rest = pl.ds(cut, ff_part - cut)
     keep_rest = pltpu.make_async_copy(
         turned.at[rest],
         turned_all.at[rest, pl.ds(pl.multiple_of(row * tokens, tokens), tokens)],
@@ -1661,15 +1663,17 @@
     for load in loads:
         load.start()
     pl.semaphore_wait(barrier, 10)
-    half_ff = ff_part // 2
+    cut = ff_part // TURNED_PART
+    spans = ((0, cut), (cut, ff_part - cut))
 
     def turned_on(part, mask):
-        rows = pl.ds(part * half_ff + (mask - 1) * (half_ff // 2), half_ff // 2)
+        begin, size = spans[part][0], spans[part][1] // 2
+        rows = pl.ds(begin + (mask - 1) * size, size)
         first = pl.multiple_of((row ^ (3 - mask)) * tokens, tokens)
         if part == 0:
             source = turned_in.at[rows, pl.ds(first, tokens)]
         else:
-            source = turned_near.at[2 - mask, pl.ds((mask - 1) * (half_ff // 2), half_ff // 2)]
+            source = turned_near.at[2 - mask, pl.ds((mask - 1) * size, size)]
         lane = part * 2 + mask - 1
         return remote(
             source,
@@ -1682,7 +1686,7 @@
     def turned_over(mask):
         return remote(
             turned_in.at[
-                pl.ds(half_ff, half_ff), pl.ds(pl.multiple_of(row * tokens, tokens), tokens)
+                pl.ds(*spans[1]), pl.ds(pl.multiple_of(row * tokens, tokens), tokens)
             ],
             turned_near.at[mask - 1],
             row_sems.at[0, 3 + mask],
@@ -1771,7 +1775,7 @@
 
     small(0, rank, mm_tn(gp_low, d_pp_low))
     small(1, rank, mm_tn(d_pg_low, h_low))
-    gather_ff.forward([lambda: None, turned_rest])
+    gather_ff.forward([lambda: None, lambda: None, turned_rest])
     gather_ff.finish()
 
     part_rows = tokens // 2
@@ -1848,7 +1852,7 @@
             source = turned_far if mask else turned_in.at[:, cols]
             target = vd.at[:, cols]
         else:
-            rows = pl.ds(part * half_ff, half_ff)
+            rows = pl.ds(*spans[part])
             source = turned_near.at[mask - 1] if part else turned_in.at[rows, cols]
             target = vd.at[rows, cols]
         return pltpu.make_async_copy(source, target, turned_sems.at[lane])
@@ -2315,7 +2319,7 @@
         shape((6, block // 2, ff_part), BF),
         shape((6, block // 2, ff_part), BF),
         shape((ff_part, tokens), BF),
-        shape((2, ff_part // 2, tokens), BF),
+        shape((2, ff_part - ff_part // TURNED_PART, tokens), BF),
     ]
     scratch = [
         vmem((width, head_dim), BF),

time: 372 us -> 371 us (level)
  no operation moved by 1% of the time
where the time goes in v1:
time: 371 us; the launch traced here: 366 us
  Pallas kernels  365 us (98%)
    pallas_call x1, Pallas kernels, run_backward(): pl.pallas_call(backward_kernel, out_shape=outs, in_specs=[vm] * 21 + [hbm...  183 us
    pallas_call x1, Pallas kernels, run_forward(): pl.pallas_call(forward_kernel, out_shape=outs, in_specs=[vm, vm, vm, hbm,...  173 us
    pallas_call x1, Pallas kernels, run_finish(): pl.pallas_call(finish_kernel, grid=(steps,), out_shape=[tokens_shape, tok...  9.02 us

profile of v1, /device:TPU:1, one launch (start us, length us, event | category | flops | bytes accessed | tf_op | source)
XLA Modules:
  0.0 366.1 jit_solution(11694112260022620852)
XLA Ops:
  0.7 173.1 %shard_map.288 = (bf16[64,2048]{1,0:T(8,128)(2,1)}, bf16[64,2048]{1,0:T(8,128)(2,1)}, f32[8,2048]{1,0:T(8,128)}, f32[512,256]{1,0:T(8,128)}, f32[512,256]{1,0:T(...) custom-call(bf16[4,64,512]{2,1,0:T(8,128)(2,1)} %bitcast.5, ...), custom_call_target="tpu_custom_call" | custom-call | flops 20000000000 | bytes 50000000 | tf_op jit(solution)/shard_map/pallas_call | solution.py:1406
  173.8 183.0 %shard_map.289 = (bf16[4,64,512]{2,1,0:T(8,128)(2,1)}, bf16[4,64,512]{2,1,0:T(8,128)(2,1)}, f32[8,512]{1,0:T(8,128)}, f32[8,128]{1,0:T(8,128)}, bf16[2,4,320,128...) custom-call(bf16[64,2048]{1,0:T(8,128)(2,1)} %get-tuple-element.73.x, ...), custom_call_target="tpu_custom_call" | custom-call | flops 40000000000 | bytes 100000000 | tf_op jit(solution)/shard_map/pallas_call | solution.py:2387
  356.8 9.0 %shard_map.290 = (bf16[2,128,512]{2,1,0:T(8,128)(2,1)}, bf16[2,128,512]{2,1,0:T(8,128)(2,1)}, f32[512,512]{1,0:T(8,128)}, f32[512,128]{1,0:T(8,128)}, f32[512,12...) custom-call(bf16[4,64,512]{2,1,0:T(8,128)(2,1)} %get-tuple-element.1, ...), custom_call_target="tpu_custom_call" | custom-call | flops 10000000 | bytes 30000000 | tf_op jit(solution)/shard_map/pallas_call | solution.py:2508
